TPU v7x, 128 devices: a whole 4x4x4 slice. The times are simulated.
128 devices in a mesh: shell: 8 (over y, z_hi), blk: 16 (over z_lo, x, core).
Axes of the slice: x: 4, y: 4, z: 4 (z_hi: 2, z_lo: 2; z = z_hi * 2 + z_lo), core: 2. Of those that a mesh axis runs over, the one named last changes fastest.
Arguments:
- cotangent: float32 [2, 256, 256, 128], P(None, 'blk', 'shell'), may hold values from -6 to 6
- bessel: float32 [256, 128, 128], P('shell'), may hold values from -0.5 to 0.5
- cycle_index: int32 [2048], replicated, may hold values from 0 to 2048
- mode_order: int32 [256], replicated, may hold values from 0 to 255, each once
Outputs:
- shell_maps: bfloat16 [128, 2048, 4096], P('shell', 'blk')
Inputs may be any that keep to these rules, and one draw needn't show every extreme that they name: `mode_order`: every slot names a different order. `cycle_index`: cycle numbers may repeat.
All inputs are finite; a program needn't handle non-finite values.
Results may differ from a plain program's by a relative error of at most 0.015.
Values may be sent and summed in bfloat16 or wider, within the bound.
A program may use at most 192 MiB of HBM per device.

v0:
```python
import math

import jax
import jax.numpy as jnp
from jax import lax
from jax.sharding import PartitionSpec as P

L = 256
NSIDE = 1024
NPHI = 4096


def legendre_table(orders, heights, degrees):
    order_int = orders[:, None]
    order_float = order_int.astype(jnp.float32)
    height = heights[None, :]
    log_start = 0.5 * (
        jnp.log((2.0 * order_float + 1.0) / (4.0 * math.pi))
        + lax.lgamma(order_float + 0.5)
        - 0.5 * math.log(math.pi)
        - lax.lgamma(order_float + 1.0)
    ) + 0.5 * order_float * jnp.log(1.0 - height * height)
    start_value = jnp.exp(log_start)
    degree_run = 16

    def advance_block(carry, first_degree):
        previous, earlier = carry
        values_list = []
        for offset in range(degree_run):
            degree = first_degree + offset
            degree_float = degree.astype(jnp.float32)
            numer = jnp.maximum(4.0 * degree_float * degree_float - 1.0, 1.0)
            denom = jnp.maximum(degree_float * degree_float - order_float * order_float, 1.0)
            factor_a = jnp.sqrt(numer / denom)
            lower = degree_float - 1.0
            factor_b = jnp.sqrt(
                jnp.maximum(lower * lower - order_float * order_float, 0.0)
                / jnp.maximum(4.0 * lower * lower - 1.0, 1.0)
            )
            recurred = factor_a * (height * previous - factor_b * earlier)
            value = jnp.where(
                degree < order_int,
                jnp.zeros_like(recurred),
                jnp.where(degree == order_int, start_value, recurred),
            )
            earlier = previous
            previous = value
            values_list.append(value)
        return ((previous, earlier), jnp.stack(values_list))

    zeros = jnp.zeros_like(start_value)
    _, blocks = lax.scan(
        advance_block, (zeros, zeros), jnp.arange(0, degrees, degree_run, dtype=jnp.int32)
    )
    return blocks.reshape((degrees,) + start_value.shape)


def rotate(field_arrays, orders, cycles):
    parity = (cycles + 1) % 2
    angle = (orders[:, None] * parity[None, :]).astype(jnp.float32) * (math.pi / NPHI)
    cosine = jnp.cos(angle)
    sine = jnp.sin(angle)
    real_part = field_arrays[:, 0] * cosine - field_arrays[:, 1] * sine
    imag_part = field_arrays[:, 0] * sine + field_arrays[:, 1] * cosine
    return jnp.stack([real_part, imag_part], axis=1)


def synthesis_table(mode_order):
    pixels = jnp.arange(NPHI, dtype=jnp.int32)
    phase_position = mode_order[:, None] * pixels[None, :] % NPHI
    angle = phase_position.astype(jnp.float32) * (2.0 * math.pi / NPHI)
    weight = (jnp.where(mode_order == 0, 1.0, 2.0) * (2.0 / L)).astype(jnp.float32)[:, None]
    return jnp.stack([weight * jnp.cos(angle), -weight * jnp.sin(angle)]).astype(jnp.bfloat16)


def harmonic(spectrum_list, orders, cycles):
    heights = (2.0 * NSIDE - 2.0 * cycles.astype(jnp.float32)) / (3.0 * NSIDE)
    legendre_rows = legendre_table(orders, heights, spectrum_list.shape[2])
    legendre_upper = legendre_rows.astype(jnp.bfloat16)
    legendre_bottom = (legendre_rows - legendre_upper.astype(jnp.float32)).astype(jnp.bfloat16)
    field_arrays = jnp.einsum(
        "pzh,ezpi->iezh", legendre_upper, spectrum_list, preferred_element_type=jnp.float32
    )
    field_arrays = field_arrays + jnp.einsum(
        "pzh,ezpi->iezh", legendre_bottom, spectrum_list, preferred_element_type=jnp.float32
    )
    return rotate(field_arrays, orders, cycles).astype(jnp.bfloat16)


def synthesize(rotated, table):
    maps = jnp.einsum("scmr,cmj->srj", rotated, table, preferred_element_type=jnp.float32)
    return maps.astype(jnp.bfloat16)


def per_device(cotangent, bessel, cycle_index, mode_order):
    partial_coeffs = jnp.einsum(
        "cmlk,lks->cmls", cotangent, bessel, precision=lax.Precision.HIGHEST
    ).astype(jnp.bfloat16)
    spectrum_list = lax.all_to_all(partial_coeffs, "shell", split_axis=3, concat_axis=2, tiled=True)
    table = synthesis_table(mode_order)
    cycle_count = cycle_index.shape[0] // lax.axis_size("blk")
    own_cycles = lax.dynamic_slice_in_dim(
        cycle_index, lax.axis_index("blk") * cycle_count, cycle_count
    )
    rotated = harmonic(
        lax.all_gather(spectrum_list, "blk", axis=1, tiled=True), mode_order, own_cycles
    )
    result = synthesize(rotated, table)
    return result


def solution(mesh):
    return jax.shard_map(
        per_device,
        mesh=mesh,
        in_specs=(P(None, "blk", "shell", None), P("shell", None, None), P(), P()),
        out_specs=P("shell", "blk", None),
        check_vma=False,
    )
```

profile of v0, /device:TPU:1, one launch (start us, length us, event | category | flops | bytes accessed | tf_op | source)
XLA Modules:
  0.0 690.9 jit_solution(4057049037057330061)
XLA Ops:
  8.3 1.9 fusion.79
  13.5 8.3 %all-to-all-start = ((bf16[8,2,8192]{2,1,0:T(2,128)(2,1)}), bf16[8,2,8192]{2,1,0:T(2,128)(2,1)S(1)}, u32[]{:S(2)}, u32[]{:S(2)}) async-start(bf16[8,2,8192]{2,1,0:T(2,128)(2,1)} %reshape.1261), calls=%async_computation | async-start | bytes 524288 | tf_op jit(solution)/shard_map/all_to_all | solution.py:99
  23.3 6.0 all-to-all-done
  32.0 543.2 %while.18 = (s32[]{:T(128)}, f32[256,128]{1,0:T(8,128)S(1)}, f32[256,128]{1,0:T(8,128)S(1)}, f32[16,16,256,128]{3,2,1,0:T(8,128)}, s32[16]{0:T(128)S(1)}, /*inde...) while((s32[]{:T(128)}, f32[256,128]{1,0:T(8,128)S(1)}, ...), condition=%wide.region_1.2_spmd.clone, body=%wide.region_0.1_spmd.clone.sunk | while | flops 9797841 | bytes 12264917 | solution.py:52
  50.2 1.7 bitcast_dynamic-update-slice_fusion.39
  51.9 1.7 bitcast_dynamic-update-slice_fusion.40
  62.8 3.2 bitcast_dynamic-update-slice_fusion.50
  84.2 1.7 bitcast_dynamic-update-slice_fusion.39
  85.8 1.7 bitcast_dynamic-update-slice_fusion.40
  96.8 3.1 bitcast_dynamic-update-slice_fusion.50
  118.1 1.7 bitcast_dynamic-update-slice_fusion.39
  119.7 1.7 bitcast_dynamic-update-slice_fusion.40
  130.7 3.1 bitcast_dynamic-update-slice_fusion.50
  152.0 1.7 bitcast_dynamic-update-slice_fusion.39
  153.7 1.7 bitcast_dynamic-update-slice_fusion.40
  164.6 3.1 bitcast_dynamic-update-slice_fusion.50
  186.0 1.7 bitcast_dynamic-update-slice_fusion.39
  187.6 1.7 bitcast_dynamic-update-slice_fusion.40
  198.6 3.2 bitcast_dynamic-update-slice_fusion.50
  220.0 1.7 bitcast_dynamic-update-slice_fusion.39
  221.6 1.7 bitcast_dynamic-update-slice_fusion.40
  232.6 3.1 bitcast_dynamic-update-slice_fusion.50
  253.9 1.7 bitcast_dynamic-update-slice_fusion.39
  255.5 1.7 bitcast_dynamic-update-slice_fusion.40
  266.5 3.2 bitcast_dynamic-update-slice_fusion.50
  289.5 1.7 bitcast_dynamic-update-slice_fusion.40
  300.5 3.1 bitcast_dynamic-update-slice_fusion.50
  323.5 1.7 bitcast_dynamic-update-slice_fusion.40
  334.4 3.1 bitcast_dynamic-update-slice_fusion.50
  357.4 1.7 bitcast_dynamic-update-slice_fusion.40
  368.4 3.1 bitcast_dynamic-update-slice_fusion.50
  391.3 1.7 bitcast_dynamic-update-slice_fusion.40
  402.3 3.1 bitcast_dynamic-update-slice_fusion.50
  425.3 1.7 bitcast_dynamic-update-slice_fusion.40
  436.2 3.1 bitcast_dynamic-update-slice_fusion.50
  459.2 1.7 bitcast_dynamic-update-slice_fusion.40
  470.2 3.2 bitcast_dynamic-update-slice_fusion.50
  493.2 1.7 bitcast_dynamic-update-slice_fusion.40
  504.2 3.1 bitcast_dynamic-update-slice_fusion.50
  527.1 1.7 bitcast_dynamic-update-slice_fusion.40
  538.1 3.1 bitcast_dynamic-update-slice_fusion.50
  561.1 1.7 bitcast_dynamic-update-slice_fusion.40
  572.0 3.1 bitcast_dynamic-update-slice_fusion.50
  576.5 19.0 %multiply_convert_fusion.1 = (bf16[1,256,4096]{2,1,0:T(8,128)(2,1)}, bf16[1,256,4096]{2,1,0:T(8,128)(2,1)}) fusion(s32[256]{0:T(256)S(1)} %bitcast.323, f32[256]{0:T(256)S(1)} %get-tuple-element.379, f32[256]{0:T(256)S(1)} %get-tuple-element.376), kind=kLoop, calls=%fused_computation.135 | loop fusion | flops 18874368 | bytes 4197376 | tf_op jit(solution)/shard_map/convert
  595.4 34.1 %fusion.37 = f32[256,2,16,128]{3,2,1,0:T(8,128)} fusion(bf16[2,256,256,16]{2,3,0,1:T(8,128)(2,1)} %all-gather.2.cloned.1.call-done, f32[256,256,128]{2,1,0:T(8,128)} %bitcast.213), kind=kOutput, calls=%fused_computation.122 | convolution fusion | flops 536870912 | bytes 41943040 | tf_op jit(solution)/shard_map/pzh,ezpi->iezh/dot_general | solution.py:81
  629.6 35.1 %add_bitcast_fusion = f32[16,2,256,128]{3,0,1,2:T(8,128)} fusion(f32[256,2,16,128]{3,2,1,0:T(8,128)} %fusion.37, bf16[2,256,256,16]{2,3,0,1:T(8,128)(2,1)} %all-gather.2.cloned.1.call-done, f32[256,256,128]{2,1,0:T(8,128)} %bitcast.214), kind=kOutput, calls=%fused_computation.138 | convolution fusion | flops 571473920 | bytes 46137344 | tf_op jit(solution)/shard_map/pzh,ezpi->iezh/dot_general | solution.py:84
  664.7 2.8 subtract_convert_fusion.1
  669.7 13.9 %bitcast_convert_fusion = bf16[16,128,4096]{2,1,0:T(8,128)(2,1)} fusion(bf16[1,256,4096]{2,1,0:T(8,128)(2,1)S(1)} %copy-done.3, bf16[1,256,4096]{2,1,0:T(8,128)(2,1)S(1)} %copy-done.2, bf16[16,2,256,128]{3,0,1,2:T(8,128)(2,1)S(1)} %pad_maximum_fusion), kind=kOutput, calls=%fused_computation.118 | convolution fusion | flops 8600420352 | bytes 23068672 | tf_op jit(solution)/shard_map/scmr,cmj->srj/dot_general | solution.py:91
  (358 shorter events, 298.2 us)
Async XLA Ops:
  6.5 1.7 copy-start
  10.2 13.0 %copy-start.4 = (s32[256]{0:T(256)S(1)}, s32[256]{0:T(256)}, u32[]{:S(2)}) copy-start(s32[256]{0:T(256)} %param.9) | copy-start | bytes 3076
  13.5 15.8 %all-to-all-start = ((bf16[8,2,8192]{2,1,0:T(2,128)(2,1)}), bf16[8,2,8192]{2,1,0:T(2,128)(2,1)S(1)}, u32[]{:S(2)}, u32[]{:S(2)}) async-start(bf16[8,2,8192]{2,1,0:T(2,128)(2,1)} %reshape.1261), calls=%async_computation | async-start | bytes 524288 | tf_op jit(solution)/shard_map/all_to_all | solution.py:99
  21.9 573.6 %all-gather.2.cloned.1.call-start = ((), (), s32[]{:S(2)}) async-start(), calls=%async_computation.1 | async-start | bytes 4456448 | tf_op jit(solution)/shard_map/all_gather | solution.py:106
  667.5 1.6 copy-start.2
  667.5 2.2 copy-start.3
  669.7 13.9 %copy-start.1 = (f32[32,128,128]{2,1,0:T(8,128)S(1)}, f32[32,128,128]{2,1,0:T(8,128)}, u32[]{:S(2)}) copy-start(f32[32,128,128]{2,1,0:T(8,128)} %param.7) | copy-start | bytes 6291460
Sparse Core Ops, SparseCore 0:
  32.1 36.7 all-gather.1
where the time goes:
time: 699 us; the launch traced here: 691 us
  other arithmetic  339 us (48%)
  loops' own time  169 us (24%)
  matrix products  85 us (12%)
  local copies, waits for them, and re-layouts  69 us (10%)
  between operations  14 us (2%)
  starting transfers between devices  8.89 us (1%)
    while x240, other arithmetic  283 us
    another operation x1, loops' own time, legendre_table(): lax.scan(advance_block, (zeros, zeros), jnp.arange(0, degrees, degree_run...  169 us
    dynamic_update_slice x16, local copies, waits for them, and re-layouts, legendre_table(): lax.scan(advance_block, (zeros, zeros), jnp.arange(0, degrees, degree_run...  50.1 us
    dot_general x1, matrix products, harmonic(): jnp.einsum('pzh,ezpi->iezh', legendre_bottom, spectrum_list, preferred_el...  35.1 us
    dot_general x1, matrix products, harmonic(): jnp.einsum('pzh,ezpi->iezh', legendre_upper, spectrum_list, preferred_ele...  34.1 us
    another operation x2, other arithmetic  21.8 us
    another operation x16, other arithmetic, advance_block(): return ((previous, earlier), jnp.stack(values_list))  17 us
  transfers between devices with their start and end apart: 2, of which 1 were waited for; matrix products, arithmetic and copies ran while one was open for 57% of the time, Pallas kernels for 0%

commit v1 on v0

v1 whole, which is shorter than its diff:
```python
import math

import jax
import jax.numpy as jnp
import numpy as np
from jax import lax
from jax.experimental import pallas as pl
from jax.experimental.pallas import tpu as pltpu
from jax.sharding import PartitionSpec as P

L = 256
M = 256
NSIDE = 1024
NPHI = 4096
ROWS = 128
SH = 16
MB = 32
LC = 16


def start_norms():
    m = range(M)
    value = [
        0.5 * (math.log((2 * k + 1) / (4 * math.pi)) + math.lgamma(k + 0.5) - math.lgamma(0.5) - math.lgamma(k + 1.0))
        for k in m
    ]
    return np.broadcast_to(np.array(value, np.float32)[:, None], (M, ROWS))


def legendre_rows(cycles, start_ref, step_ref):
    x = (2.0 * NSIDE - 2.0 * cycles.astype(jnp.float32)) / (3.0 * NSIDE)
    degree = lax.broadcasted_iota(jnp.int32, (L, ROWS), 0).astype(jnp.float32)
    root = jnp.sqrt(jnp.maximum(4.0 * degree * degree - 1.0, 1.0))
    lower = degree - 1.0
    root_lower = jnp.sqrt(jnp.maximum(4.0 * lower * lower - 1.0, 1.0))
    start_ref[...] = root * x
    step_ref[...] = root / root_lower
    return jnp.log(1.0 - x * x)


def legendre_block(block, log_height, norm_ref, x_ref, step_ref, stage_ref, table_ref):
    first = block * MB
    groups = MB // 8
    sub = lax.broadcasted_iota(jnp.int32, (8, ROWS), 0)
    orders = [(first + 8 * g + sub) for g in range(groups)]
    order_f = [o.astype(jnp.float32) for o in orders]
    square = [o * o for o in order_f]
    start = [
        jnp.exp(norm_ref[pl.ds(pl.multiple_of(first + 8 * g, 8), 8), :] + 0.5 * order_f[g] * log_height)
        for g in range(groups)
    ]

    def clear(k, _):
        for i in range(MB):
            table_ref[first + i, pl.ds(pl.multiple_of(k * LC, LC), LC), :] = jnp.zeros((LC, ROWS), jnp.bfloat16)
        return 0

    lax.fori_loop(0, first // LC, clear, 0)

    def chunk(k, carry, starting):
        prev, earlier, root_prev = carry
        base = pl.multiple_of(k * LC, LC)
        for j in range(LC):
            degree = base + j
            degree_f = degree.astype(jnp.float32)
            x_row = x_ref[pl.ds(degree, 1), :]
            step_row = step_ref[pl.ds(degree, 1), :]
            new, root_new = [], []
            for g in range(groups):
                d = degree_f * degree_f - square[g]
                inv = lax.rsqrt(jnp.maximum(d, 1.0) if starting else d)
                value = inv * (x_row * prev[g] - (step_row * root_prev[g]) * earlier[g])
                if starting:
                    value = jnp.where(orders[g] == degree, start[g], value)
                stage_ref[pl.ds(8 * g * LC + j, 8, stride=LC), :] = value
                new.append(value)
                root_new.append(d * inv)
            earlier, prev, root_prev = prev, new, root_new
        for i in range(MB):
            table_ref[first + i, pl.ds(base, LC), :] = stage_ref[i * LC:(i + 1) * LC, :].astype(jnp.bfloat16)
        return prev, earlier, root_prev

    zeros = [jnp.zeros((8, ROWS), jnp.float32)] * groups
    carry = (zeros, zeros, zeros)
    lo = first // LC
    carry = lax.fori_loop(lo, lo + MB // LC, lambda k, c: chunk(k, c, True), carry)
    lax.fori_loop(lo + MB // LC, L // LC, lambda k, c: chunk(k, c, False), carry)


def turn_tables(cycles, cos_ref, sin_ref):
    odd = (lax.rem(cycles + 1, 2) == 1)
    order = lax.broadcasted_iota(jnp.int32, (M, ROWS), 0).astype(jnp.float32)
    a = order * (math.pi / NPHI)
    q = a * a
    cosine = 1.0 - q * (0.5 - q * (1.0 / 24 - q * (1.0 / 720)))
    sine = a * (1.0 - q * (1.0 / 6 - q * (1.0 / 120 - q * (1.0 / 5040))))
    cos_ref[...] = jnp.where(odd, cosine, 1.0)
    sin_ref[...] = jnp.where(odd, sine, 0.0)


def field_of(order, coeffs, table_ref, cos_ref, sin_ref):
    f = jnp.dot(coeffs, table_ref[order], preferred_element_type=jnp.float32)
    c = cos_ref[pl.ds(order, 1), :]
    s = sin_ref[pl.ds(order, 1), :]
    fr, fi = f[:SH], f[SH:]
    return (fr * c - fi * s).astype(jnp.bfloat16), (fr * s + fi * c).astype(jnp.bfloat16)


def fields_kernel(mode_ref, cyc_ref, norm_ref, coeff_ref, out_ref, x_ref, step_ref, stage_ref, table_ref, cos_ref, sin_ref):
    own = lax.axis_index("blk")
    cycles = cyc_ref[pl.ds(own, 1), :]
    log_height = legendre_rows(cycles, x_ref, step_ref)
    turn_tables(cycles, cos_ref, sin_ref)

    def block(k, _):
        legendre_block(k, log_height, norm_ref, x_ref, step_ref, stage_ref, table_ref)
        return 0

    lax.fori_loop(0, M // MB, block, 0)

    def slots(k, _):
        for u in range(8):
            t = k * 8 + u
            re, im = field_of(mode_ref[t], coeff_ref[t], table_ref, cos_ref, sin_ref)
            out_ref[t, :SH, :] = re
            out_ref[t, SH:, :] = im
        return 0

    lax.fori_loop(0, M // 8, slots, 0)


SPS = 2
JC = 512


def twiddles(tab_ref):
    half = M // 2
    for par in range(2):
        order = 2 * lax.broadcasted_iota(jnp.int32, (half, 128), 0) + par
        pixel = lax.broadcasted_iota(jnp.int32, (half, 128), 1)
        w = jnp.where(order == 0, 2.0 / L, 4.0 / L)
        angle = lax.rem(order * pixel, NPHI).astype(jnp.float32) * (2.0 * math.pi / NPHI)
        turn = lax.rem(order * 128, NPHI).astype(jnp.float32) * (2.0 * math.pi / NPHI)
        c, s = w * jnp.cos(angle), w * jnp.sin(angle)
        tc, ts = jnp.cos(turn), jnp.sin(turn)
        for j in range(NPHI // 2 // 128):
            tab_ref[par, :half, j * 128:(j + 1) * 128] = c.astype(jnp.bfloat16)
            tab_ref[par, half:, j * 128:(j + 1) * 128] = (-s).astype(jnp.bfloat16)
            c, s = c * tc - s * ts, s * tc + c * ts


def maps_kernel(mode_ref, f_ref, out_ref, g_ref, tab_ref):
    half = M // 2

    @pl.when(pl.program_id(0) == 0)
    def _():
        twiddles(tab_ref)

        def place(k, _):
            for u in range(8):
                t = k * 8 + u
                m = mode_ref[t]
                row = lax.rem(m, 2) * M + m // 2
                v = f_ref[t].astype(jnp.float32)
                g_ref[pl.ds(row, SH, stride=2 * M), :] = v[:SH]
                g_ref[pl.ds(row + half, SH, stride=2 * M), :] = v[SH:]
            return 0

        lax.fori_loop(0, M // 8, place, 0)

    first = pl.program_id(0) * SPS
    even, odd = [], []
    for i in range(SPS):
        base = pl.multiple_of((first + i) * 2 * M, 2 * M)
        even.append(g_ref[pl.ds(base, M), :].T.astype(jnp.bfloat16))
        odd.append(g_ref[pl.ds(base + M, M), :].T.astype(jnp.bfloat16))
    even = jnp.concatenate(even, axis=0)
    odd = jnp.concatenate(odd, axis=0)
    for j in range(0, NPHI // 2, JC):
        e = jnp.dot(even, tab_ref[0, :, j:j + JC], preferred_element_type=jnp.float32)
        o = jnp.dot(odd, tab_ref[1, :, j:j + JC], preferred_element_type=jnp.float32)
        p = (e + o).astype(jnp.bfloat16)
        q = (e - o).astype(jnp.bfloat16)
        for i in range(SPS):
            out_ref[i, :, j:j + JC] = p[i * ROWS:(i + 1) * ROWS]
            out_ref[i, :, NPHI // 2 + j:NPHI // 2 + j + JC] = q[i * ROWS:(i + 1) * ROWS]


def maps_call(mode_order, fields):
    return pl.pallas_call(
        maps_kernel,
        out_shape=jax.ShapeDtypeStruct((SH, ROWS, NPHI), jnp.bfloat16),
        grid_spec=pltpu.PrefetchScalarGridSpec(
            num_scalar_prefetch=1,
            grid=(SH // SPS,),
            in_specs=[pl.BlockSpec((M, 2 * SH, ROWS), lambda i, m: (0, 0, 0))],
            out_specs=pl.BlockSpec((SPS, ROWS, NPHI), lambda i, m: (i, 0, 0)),
            scratch_shapes=[
                pltpu.VMEM((SH * 2 * M, ROWS), jnp.float32),
                pltpu.VMEM((2, M, NPHI // 2), jnp.bfloat16),
            ],
        ),
        compiler_params=pltpu.CompilerParams(vmem_limit_bytes=40 << 20),
        name="maps",
    )(mode_order, fields)


def fields_call(mode_order, cycle_index, coeffs):
    vmem = pl.BlockSpec(memory_space=pltpu.VMEM)
    return pl.pallas_call(
        fields_kernel,
        out_shape=jax.ShapeDtypeStruct((M, 2 * SH, ROWS), jnp.bfloat16),
        in_specs=[pl.BlockSpec(memory_space=pltpu.SMEM), vmem, vmem, vmem],
        out_specs=vmem,
        scratch_shapes=[
            pltpu.VMEM((L, ROWS), jnp.float32),
            pltpu.VMEM((L, ROWS), jnp.float32),
            pltpu.VMEM((MB * LC, ROWS), jnp.float32),
            pltpu.VMEM((M, L, ROWS), jnp.bfloat16),
            pltpu.VMEM((M, ROWS), jnp.float32),
            pltpu.VMEM((M, ROWS), jnp.float32),
        ],
        compiler_params=pltpu.CompilerParams(vmem_limit_bytes=50 << 20),
        name="fields",
    )(mode_order, cycle_index.reshape(-1, ROWS), jnp.asarray(start_norms()), coeffs)


def per_device(cotangent, bessel, cycle_index, mode_order):
    coeffs = jnp.einsum("cmlk,lks->cmls", cotangent, bessel).astype(jnp.bfloat16)
    coeffs = lax.all_to_all(coeffs, "shell", split_axis=3, concat_axis=2, tiled=True)
    coeffs = jnp.transpose(coeffs, (1, 0, 3, 2)).reshape(-1, 2 * SH, L)
    coeffs = lax.all_gather(coeffs, "blk", axis=0, tiled=True)
    return maps_call(mode_order, fields_call(mode_order, cycle_index, coeffs))


def solution(mesh):
    return jax.shard_map(
        per_device,
        mesh=mesh,
        in_specs=(P(None, "blk", "shell", None), P("shell", None, None), P(), P()),
        out_specs=P("shell", "blk", None),
        check_vma=False,
    )
```

time: 699 us -> 114 us (0.16); the launches traced: 691 us -> 114 us
  other arithmetic: 339 us -> 0.04 us
  loops' own time: 169 us -> 0 us
  matrix products: 85 us -> 0.39 us
  local copies, waits for them, and re-layouts: 69 us -> 10.7 us
  Pallas kernels: 0 us -> 36.7 us
  waiting for transfers between devices: 6 us -> 37 us
  blocking collectives: 0 us -> 15.7 us
  starting transfers between devices: 8.89 us -> 0.01 us
    while x240 -> x0, other arithmetic: 283 us -> none
    another operation x1 -> x0, loops' own time: 169 us -> none  [legendre_table(): lax.scan(advance_block, (zeros, zeros), jnp.arange(0, degrees, degree_run...]
    dot_general x3 -> x0, matrix products: 83.1 us -> none  [the longest x1 35.1 us: harmonic(): jnp.einsum('pzh,ezpi->iezh', legendre_bottom, spectrum_list, preferred_el...]
    dynamic_update_slice x16 -> x0, local copies, waits for them, and re-layouts: 50.1 us -> none  [legendre_table(): lax.scan(advance_block, (zeros, zeros), jnp.arange(0, degrees, degree_run...]
    another operation x19 -> x0, other arithmetic: 39 us -> none
    all_gather x1, waiting for transfers between devices: 0.01 us -> 37 us  [per_device(): coeffs = lax.all_gather(coeffs, 'blk', axis=0, tiled=True)]
    pallas_call x0 -> x2, Pallas kernels: none -> 36.7 us  [the longest x1 21.3 us: fields_call(): pl.pallas_call(fields_kernel, out_shape=jax.ShapeDtypeStruct((M, 2 * SH,...]
    all_to_all x0 -> x1, blocking collectives: none -> 15.7 us  [per_device(): lax.all_to_all(coeffs, 'shell', split_axis=3, concat_axis=2, tiled=True)]
  transfers between devices with their start and end apart: 2 -> 1, of which waited for: 1 -> 1; matrix products, arithmetic and copies ran while one was open for 57% -> 0% of each run, Pallas kernels for 0% -> 0%
where the time goes in v1:
time: 114 us
  waiting for transfers between devices  37 us (32%)
  Pallas kernels  36.7 us (32%)
  blocking collectives  15.7 us (14%)
  between operations  13.5 us (12%)
  local copies, waits for them, and re-layouts  10.7 us (9%)
    all_gather x1, waiting for transfers between devices, per_device(): coeffs = lax.all_gather(coeffs, 'blk', axis=0, tiled=True)  37 us
    pallas_call x1, Pallas kernels, fields_call(): pl.pallas_call(fields_kernel, out_shape=jax.ShapeDtypeStruct((M, 2 * SH,...  21.3 us
    all_to_all x1, blocking collectives, per_device(): lax.all_to_all(coeffs, 'shell', split_axis=3, concat_axis=2, tiled=True)  15.7 us
    pallas_call x1, Pallas kernels, maps_call(): pl.pallas_call(maps_kernel, out_shape=jax.ShapeDtypeStruct((SH, ROWS, NPH...  15.4 us
    unnamed x11, local copies, waits for them, and re-layouts  4.65 us
    all_to_all x2, local copies, waits for them, and re-layouts, per_device(): lax.all_to_all(coeffs, 'shell', split_axis=3, concat_axis=2, tiled=True)  3.66 us
  transfers between devices with their start and end apart: 1, of which 1 were waited for; matrix products, arithmetic and copies ran while one was open for 0% of the time, Pallas kernels for 0%

profile of v1, /device:TPU:1, one launch (start us, length us, event | category | flops | bytes accessed | tf_op | source)
XLA Modules:
  0.0 114.1 jit_solution(14786404700836865539)
XLA Ops:
  6.5 0.0 copy-start
  6.5 0.0 all-gather.2.cloned.1.call-start
  6.5 1.5 %copy.23 = bf16[2,16,32,128]{3,1,0,2:T(8,128)(2,1)S(1)} copy(f32[2,16,32,128]{3,2,1,0:T(8,128)} %param.5) | data formatting | bytes 786432 | tf_op args[0]
  8.0 0.2 copy-done
  8.3 0.4 fusion
  8.7 1.6 %copy.24 = bf16[2,16,32,128]{2,1,0,3:T(8,128)(2,1)S(1)} copy(bf16[2,16,32,128]{3,1,0,2:T(8,128)(2,1)S(1)} %convert_bitcast_fusion) | data formatting | bytes 524288 | tf_op jit(solution)/shard_map/convert_element_type | solution.py:229
  10.3 1.0 reshape.10
  11.3 15.7 %all_to_all.18 = bf16[8,2,8192]{2,1,0:T(2,128)(2,1)} all-to-all(bf16[8,2,8192]{2,1,0:T(2,128)(2,1)S(1)} %reshape.10), channel_id=1, replica_groups=mesh['shell'=8,'blk'=16] {'shell'}, dimensions={0} | all-to-all | bytes 524288 | tf_op jit(solution)/shard_map/all_to_all | solution.py:230
  27.0 1.9 %reshape.11 = bf16[128,2,16,32]{3,2,1,0:T(8,128)(2,1)S(1)} reshape(bf16[8,2,8192]{2,1,0:T(2,128)(2,1)} %all_to_all.18) | data formatting | bytes 524288
  28.9 0.0 copy-start.3
  28.9 0.0 copy-start.1
  28.9 0.0 copy-start.2
  28.9 1.6 %copy.26 = bf16[2,16,8,32,16]{3,2,4,1,0:T(8,128)(2,1)} copy(bf16[2,16,8,32,16]{3,1,0,4,2:T(8,128)(2,1)S(1)} %bitcast.22) | data formatting | bytes 524288 | tf_op jit(solution)/shard_map/all_to_all | solution.py:230
  30.6 2.0 %all_to_all.16 = bf16[2,16,256,16]{2,3,1,0:T(8,128)(2,1)S(1)} reshape(bf16[2,16,8,32,16]{3,2,4,1,0:T(8,128)(2,1)} %copy.26) | data formatting | bytes 524288 | tf_op jit(solution)/shard_map/all_to_all | solution.py:230
  32.6 0.7 copy.27
  33.3 0.0 all-gather.2.cloned.1.call-update
  33.4 37.0 %all-gather.2.cloned.1.call-done.coeff_ref = bf16[256,32,256]{2,1,0:T(8,128)(2,1)} async-done(((bf16[16,32,256]{2,1,0:T(8,128)(2,1)}), bf16[256,32,256]{2,1,0:T(8,128)(2,1)}) %all-gather.2.cloned.1.call-update) | async-done | bytes 4194320 | tf_op jit(solution)/shard_map/all_gather | solution.py:232
  70.4 0.0 copy-done.3
  70.4 0.1 jit_solution_.3.norm_ref
  70.5 0.0 copy-done.1
  70.5 0.0 copy-done.2
  70.5 21.3 %fields.1.f_ref = bf16[256,32,128]{2,1,0:T(8,128)(2,1)S(1)} custom-call(s32[256]{0:T(256)S(1)} %copy-done.2, s32[16,128]{1,0:T(8,128)S(1)} %bitcast.20, f32[256,128]{1,0:T(8,128)S(1)} %jit_solution_.3.norm_ref, bf16[256,32,256]{2,1,0:T(8,128)(2,1)} %all-gather.2.cloned.1.call-done.coeff_ref), custom_call_target="tpu_custom_call" | custom-call | tf_op jit(solution)/shard_map/fields/pallas_call | solution.py:210
  91.8 15.4 %maps.1 = bf16[16,128,4096]{2,1,0:T(8,128)(2,1)} custom-call(s32[256]{0:T(256)S(1)} %copy-done.2, bf16[256,32,128]{2,1,0:T(8,128)(2,1)S(1)} %fields.1.f_ref), custom_call_target="tpu_custom_call" | custom-call | tf_op jit(solution)/shard_map/maps/pallas_call | solution.py:190
  (1 shorter events, 0.0 us)
Async XLA Ops:
  6.5 1.7 %copy-start = (f32[32,128,128]{2,1,0:T(8,128)S(1)}, f32[32,128,128]{2,1,0:T(8,128)}, u32[]{:S(2)}) copy-start(f32[32,128,128]{2,1,0:T(8,128)} %param.6) | copy-start | bytes 6291460
  6.5 63.8 %all-gather.2.cloned.1.call-start = ((), (), s32[]{:S(2)}) async-start(), calls=%async_computation.1 | async-start | bytes 4456448 | tf_op jit(solution)/shard_map/all_gather | solution.py:232
  28.9 41.5 %copy-start.3 = (f32[256]{0:T(256)S(1)}, f32[256]{0:T(256)}, u32[]{:S(2)}) copy-start(f32[256]{0:T(256)} %constant.2.clone) | copy-start | bytes 3076
  28.9 41.6 %copy-start.1 = (s32[2048]{0:T(1024)S(1)}, s32[2048]{0:T(1024)}, u32[]{:S(2)}) copy-start(s32[2048]{0:T(1024)} %param.7) | copy-start | bytes 24580
  28.9 41.6 %copy-start.2 = (s32[256]{0:T(256)S(1)}, s32[256]{0:T(256)}, u32[]{:S(2)}) copy-start(s32[256]{0:T(256)} %mode_ref.3) | copy-start | bytes 3076
Sparse Core Ops, SparseCore 0:
  33.5 36.8 all-gather.1

commit v2 on v1

--- a/solution.py
+++ b/solution.py
@@ -106,27 +106,188 @@
     return (fr * c - fi * s).astype(jnp.bfloat16), (fr * s + fi * c).astype(jnp.bfloat16)
 
 
-def fields_kernel(mode_ref, cyc_ref, norm_ref, coeff_ref, out_ref, x_ref, step_ref, stage_ref, table_ref, cos_ref, sin_ref):
+GROUP = 8
+KL = L // GROUP
+SLOTS = 16
+HALF = SLOTS // 2
+WAVES = 128
+MESH = pl.DeviceIdType.MESH
+
+
+def radial(cot_ref, bes_ref, stage_ref, send_ref):
+    def degree(k, _):
+        for u in range(4):
+            l = k * 4 + u
+            c = cot_ref[pl.ds(l, 2 * SLOTS, stride=KL), :].astype(jnp.bfloat16)
+            w = bes_ref[pl.ds(pl.multiple_of(l * WAVES, WAVES), WAVES), :].astype(jnp.bfloat16)
+            stage_ref[pl.ds(l, 2 * SLOTS, stride=KL), :] = jnp.dot(c, w, preferred_element_type=jnp.float32)
+        return 0
+
+    lax.fori_loop(0, KL // 4, degree, 0)
+    for q in range(8):
+        tile = stage_ref[q * 128:(q + 1) * 128, :].T.astype(jnp.bfloat16)
+        for h in range(GROUP):
+            send_ref[h, q] = tile[h * SH:(h + 1) * SH]
+
+
+def shuffle_matrix(perm_ref):
+    k = lax.broadcasted_iota(jnp.int32, (512, 512), 0)
+    n = lax.broadcasted_iota(jnp.int32, (512, 512), 1)
+    to = lax.rem(k, 128) // 32 * 128 + k // 128 * 32 + lax.rem(k, 32)
+    perm_ref[...] = (to == n).astype(jnp.float32).astype(jnp.bfloat16)
+
+
+def relayout(recv_ref, perm_ref, own, block_ref):
+    for h in range(2):
+        x = jnp.concatenate([recv_ref[4 * h + j].reshape(128, 128) for j in range(4)], axis=1)
+        y = jnp.dot(x, perm_ref[...], preferred_element_type=jnp.float32).astype(jnp.bfloat16)
+        for q in range(8):
+            for i in range(4):
+                c, t = divmod(4 * q + i, SLOTS)
+                block_ref[own, t, c * SH:(c + 1) * SH, h * 128:(h + 1) * 128] = y[q * SH:(q + 1) * SH, i * 128:(i + 1) * 128]
+
+
+def fields_kernel(
+    mode_ref, cyc_ref, norm_ref, cot_hbm, bes_hbm, out_ref,
+    x_ref, step_ref, stage_ref, table_ref, cos_ref, sin_ref,
+    cot_ref, bes_ref, rad_ref, send_ref, recv_ref, perm_ref, block_ref,
+    load_sem, a2a_send, a2a_recv, ring_send, ring_recv,
+):
     own = lax.axis_index("blk")
+    shell = lax.axis_index("shell")
+    core = lax.rem(own, 2)
+    x = lax.rem(own // 2, 4)
+    z = own // 8
+    d = 1 - 2 * core
+
+    def at(dz, k):
+        return lax.rem(z + dz, 2) * 8 + lax.rem(x + k * d + 8, 4) * 2 + core
+
+    ahead, behind, across, sibling = at(0, 1), at(0, -1), at(1, 0), own + d
+
+    loads = [
+        pltpu.make_async_copy(cot_hbm, cot_ref, load_sem.at[0]),
+        pltpu.make_async_copy(bes_hbm, bes_ref, load_sem.at[1]),
+    ]
+    for copy in loads:
+        copy.start()
+    barrier = pltpu.get_barrier_semaphore()
+    for peer in (ahead, behind, across, sibling):
+        pl.semaphore_signal(barrier, inc=1, device_id={"blk": peer}, device_id_type=MESH)
+    for k in range(1, GROUP):
+        pl.semaphore_signal(barrier, inc=1, device_id={"shell": lax.rem(shell + k, GROUP)}, device_id_type=MESH)
+
     cycles = cyc_ref[pl.ds(own, 1), :]
     log_height = legendre_rows(cycles, x_ref, step_ref)
     turn_tables(cycles, cos_ref, sin_ref)
-
-    def block(k, _):
-        legendre_block(k, log_height, norm_ref, x_ref, step_ref, stage_ref, table_ref)
-        return 0
-
-    lax.fori_loop(0, M // MB, block, 0)
-
-    def slots(k, _):
-        for u in range(8):
-            t = k * 8 + u
-            re, im = field_of(mode_ref[t], coeff_ref[t], table_ref, cos_ref, sin_ref)
-            out_ref[t, :SH, :] = re
-            out_ref[t, SH:, :] = im
-        return 0
-
-    lax.fori_loop(0, M // 8, slots, 0)
+    shuffle_matrix(perm_ref)
+
+    def table(lo, hi):
+        def block(k, _):
+            legendre_block(k, log_height, norm_ref, x_ref, step_ref, stage_ref, table_ref)
+            return 0
+
+        lax.fori_loop(lo, hi, block, 0)
+
+    for copy in loads:
+        copy.wait()
+    radial(cot_ref, bes_ref, rad_ref, send_ref)
+    pl.semaphore_wait(barrier, 4 + GROUP - 1)
+    exchange = []
+    for k in range(1, GROUP):
+        to = lax.rem(shell + k, GROUP)
+        copy = pltpu.make_async_remote_copy(
+            src_ref=send_ref.at[to], dst_ref=recv_ref.at[shell], send_sem=a2a_send.at[k - 1], recv_sem=a2a_recv.at[k - 1],
+            device_id={"shell": to}, device_id_type=MESH,
+        )
+        copy.start()
+        exchange.append(copy)
+    recv_ref[shell] = send_ref[shell]
+    table(0, 1)
+    for k in range(1, GROUP):
+        source = lax.rem(shell - k + GROUP, GROUP)
+        pltpu.make_async_remote_copy(
+            src_ref=send_ref.at[source], dst_ref=recv_ref.at[source], send_sem=a2a_send.at[k - 1], recv_sem=a2a_recv.at[k - 1],
+            device_id={"shell": source}, device_id_type=MESH,
+        ).wait_recv()
+    relayout(recv_ref, perm_ref, own, block_ref)
+
+    sent = []
+
+    def piece(part, index):
+        return block_ref.at[index, pl.ds(HALF * part, HALF)]
+
+    def describe(part, index, to, slot):
+        return pltpu.make_async_remote_copy(
+            src_ref=piece(part, index), dst_ref=piece(part, index), send_sem=ring_send.at[slot],
+            recv_sem=ring_recv.at[part, index], device_id={"blk": to}, device_id_type=MESH,
+        )
+
+    def send(part, index, *targets):
+        for to in targets:
+            copy = describe(part, index, to, len(sent))
+            copy.start()
+            sent.append(copy)
+
+    def arrive(part, index):
+        describe(part, index, sibling, 0).wait_recv()
+
+    for part in range(2):
+        send(part, own, across, ahead, behind)
+    for part in range(2):
+        send(part, own, sibling)
+    table(1, 2)
+    arrive(0, at(1, 0))
+    send(0, at(1, 0), ahead, behind)
+    arrive(0, at(0, -1))
+    send(0, at(0, -1), ahead)
+    arrive(0, at(0, 1))
+    for index in (at(1, 0), at(0, -1), at(0, 1)):
+        send(0, index, sibling)
+    table(2, 3)
+    arrive(1, at(0, -1))
+    send(1, at(0, -1), ahead, across)
+    arrive(1, at(0, 1))
+    send(1, at(0, 1), across)
+    for index in (at(0, -1), at(0, 1)):
+        send(1, index, sibling)
+    table(3, 5)
+    arrive(0, at(1, -1))
+    send(0, at(1, -1), ahead)
+    arrive(1, at(0, 2))
+    send(1, at(0, 2), across)
+    arrive(0, at(0, 2))
+    arrive(0, at(1, 1))
+    for part, index in ((0, at(1, -1)), (1, at(0, 2)), (0, at(0, 2)), (0, at(1, 1))):
+        send(part, index, sibling)
+    table(5, 8)
+
+    def slots(index, part):
+        def step(k, _):
+            for u in range(4):
+                t = HALF * part + k * 4 + u
+                g = index * SLOTS + t
+                re, im = field_of(mode_ref[g], block_ref[index, t], table_ref, cos_ref, sin_ref)
+                out_ref[g, :SH, :] = re
+                out_ref[g, SH:, :] = im
+            return 0
+
+        lax.fori_loop(0, HALF // 4, step, 0)
+
+    ready = [(0, own), (1, own)]
+    ready += [(0, at(1, 0)), (0, at(0, -1)), (0, at(0, 1)), (1, at(0, -1)), (1, at(0, 1))]
+    ready += [(0, at(1, -1)), (1, at(0, 2)), (0, at(0, 2)), (0, at(1, 1))]
+    last = [(1, at(1, 0)), (1, at(1, -1)), (1, at(1, 1)), (0, at(1, 2)), (1, at(1, 2))]
+    for part, index in last:
+        arrive(part, index)
+        send(part, index, sibling)
+    for part, index in ready + last:
+        slots(index, part)
+    for part, index in ready + last:
+        arrive(part, index + d)
+        slots(index + d, part)
+    for copy in exchange + sent:
+        copy.wait_send()
 
 
 SPS = 2
@@ -205,12 +366,13 @@
     )(mode_order, fields)
 
 
-def fields_call(mode_order, cycle_index, coeffs):
+def fields_call(cotangent, bessel, cycle_index, mode_order):
     vmem = pl.BlockSpec(memory_space=pltpu.VMEM)
+    hbm = pl.BlockSpec(memory_space=pl.ANY)
     return pl.pallas_call(
         fields_kernel,
         out_shape=jax.ShapeDtypeStruct((M, 2 * SH, ROWS), jnp.bfloat16),
-        in_specs=[pl.BlockSpec(memory_space=pltpu.SMEM), vmem, vmem, vmem],
+        in_specs=[pl.BlockSpec(memory_space=pltpu.SMEM), vmem, vmem, hbm, hbm],
         out_specs=vmem,
         scratch_shapes=[
             pltpu.VMEM((L, ROWS), jnp.float32),
@@ -219,18 +381,30 @@
             pltpu.VMEM((M, L, ROWS), jnp.bfloat16),
             pltpu.VMEM((M, ROWS), jnp.float32),
             pltpu.VMEM((M, ROWS), jnp.float32),
+            pltpu.VMEM((2 * SLOTS * KL, WAVES), jnp.float32),
+            pltpu.VMEM((KL * WAVES, 128), jnp.float32),
+            pltpu.VMEM((2 * SLOTS * KL, 128), jnp.float32),
+            pltpu.VMEM((GROUP, 8, SH, 128), jnp.bfloat16),
+            pltpu.VMEM((GROUP, 8, SH, 128), jnp.bfloat16),
+            pltpu.VMEM((512, 512), jnp.bfloat16),
+            pltpu.VMEM((16, SLOTS, 2 * SH, L), jnp.bfloat16),
+            pltpu.SemaphoreType.DMA((2,)),
+            pltpu.SemaphoreType.DMA((GROUP - 1,)),
+            pltpu.SemaphoreType.DMA((GROUP - 1,)),
+            pltpu.SemaphoreType.DMA((30,)),
+            pltpu.SemaphoreType.DMA((2, 16)),
         ],
-        compiler_params=pltpu.CompilerParams(vmem_limit_bytes=50 << 20),
+        compiler_params=pltpu.CompilerParams(vmem_limit_bytes=50 << 20, collective_id=0, has_side_effects=True),
         name="fields",
-    )(mode_order, cycle_index.reshape(-1, ROWS), jnp.asarray(start_norms()), coeffs)
+    )(
+        mode_order, cycle_index.reshape(-1, ROWS), jnp.asarray(start_norms()),
+        cotangent.reshape(-1, WAVES), bessel.reshape(-1, 128),
+    )
 
 
 def per_device(cotangent, bessel, cycle_index, mode_order):
-    coeffs = jnp.einsum("cmlk,lks->cmls", cotangent, bessel).astype(jnp.bfloat16)
-    coeffs = lax.all_to_all(coeffs, "shell", split_axis=3, concat_axis=2, tiled=True)
-    coeffs = jnp.transpose(coeffs, (1, 0, 3, 2)).reshape(-1, 2 * SH, L)
-    coeffs = lax.all_gather(coeffs, "blk", axis=0, tiled=True)
-    return maps_call(mode_order, fields_call(mode_order, cycle_index, coeffs))
+    fields = fields_call(cotangent, bessel, cycle_index, mode_order)
+    return maps_call(mode_order, fields)
 
 
 def solution(mesh):

time: 114 us -> 62.3 us (0.55)
  waiting for transfers between devices: 37 us -> 0 us
  Pallas kernels: 36.7 us -> 58.5 us
  blocking collectives: 15.7 us -> 0 us
  between operations: 13.5 us -> 0.03 us
  local copies, waits for them, and re-layouts: 10.7 us -> 3.18 us
    all_gather x1 -> x0, waiting for transfers between devices: 37 us -> none  [per_device(): coeffs = lax.all_gather(coeffs, 'blk', axis=0, tiled=True)]
    pallas_call x1, Pallas kernels: 21.3 us -> 43.1 us  [fields_call(): pl.pallas_call(fields_kernel, out_shape=jax.ShapeDtypeStruct((M, 2 * SH,...]
    all_to_all x1 -> x0, blocking collectives: 15.7 us -> none  [per_device(): lax.all_to_all(coeffs, 'shell', split_axis=3, concat_axis=2, tiled=True)]
    all_to_all x2 -> x0, local copies, waits for them, and re-layouts: 3.66 us -> none  [per_device(): lax.all_to_all(coeffs, 'shell', split_axis=3, concat_axis=2, tiled=True)]
    unnamed x11 -> x6, local copies, waits for them, and re-layouts: 4.65 us -> 2.41 us
    convert_element_type x1 -> x0, local copies, waits for them, and re-layouts: 1.61 us -> none  [per_device(): jnp.einsum('cmlk,lks->cmls', cotangent, bessel).astype(jnp.bfloat16)]
  transfers between devices with their start and end apart: 1 -> 0, of which waited for: 1 -> 0; matrix products, arithmetic and copies ran while one was open for 0% -> 0% of each run, Pallas kernels for 0% -> 0%
where the time goes in v2:
time: 62.3 us; the launch traced here: 61.7 us
  Pallas kernels  58.5 us (94%)
  local copies, waits for them, and re-layouts  3.18 us (5%)
    pallas_call x1, Pallas kernels, fields_call(): pl.pallas_call(fields_kernel, out_shape=jax.ShapeDtypeStruct((M, 2 * SH,...  43.1 us
    pallas_call x1, Pallas kernels, maps_call(): pl.pallas_call(maps_kernel, out_shape=jax.ShapeDtypeStruct((SH, ROWS, NPH...  15.4 us
    unnamed x6, local copies, waits for them, and re-layouts  2.41 us

profile of v2, /device:TPU:1, one launch (start us, length us, event | category | flops | bytes accessed | tf_op | source)
XLA Modules:
  0.0 61.7 jit_solution(6909445527383404998)
XLA Ops:
  0.0 0.8 %jit_solution_.3.norm_ref = f32[256,128]{1,0:T(8,128)S(1)} broadcast(f32[256]{0:T(256)} %constant.2.clone), dimensions={0} | broadcast | bytes 132096 | tf_op jit(solution)
  0.8 0.0 copy-start
  0.8 1.0 %copy-done = f32[2,16,32,128]{3,2,1,0:T(8,128)S(1)} copy-done((f32[2,16,32,128]{3,2,1,0:T(8,128)S(1)}, f32[2,16,32,128]{3,2,1,0:T(8,128)}, u32[]{:S(2)}) %copy-start) | copy-done | bytes 524312
  1.8 0.0 copy-start.1
  1.8 0.7 %copy-done.1 = s32[2048]{0:T(1024)S(1)} copy-done((s32[2048]{0:T(1024)S(1)}, s32[2048]{0:T(1024)}, u32[]{:S(2)}) %copy-start.1) | copy-done | bytes 8216
  2.5 0.0 copy-start.2
  2.5 0.7 %copy-done.2 = s32[256]{0:T(256)S(1)} copy-done((s32[256]{0:T(256)S(1)}, s32[256]{0:T(256)}, u32[]{:S(2)}) %copy-start.2) | copy-done | bytes 1048
  3.2 43.1 %fields.1.f_ref = bf16[256,32,128]{2,1,0:T(8,128)(2,1)S(1)} custom-call(s32[256]{0:T(256)S(1)} %copy-done.2, s32[16,128]{1,0:T(8,128)S(1)} %bitcast.4, f32[256,128]{1,0:T(8,128)S(1)} %jit_solution_.3.norm_ref, f32[1024,128]{1,0:T(8,128)S(1)} %bitcast.3, f32[4096,128]{1,0:T(8,128)} %bitcast.5), custom_call_target="tpu_custom_call" | custom-call | tf_op jit(solution)/shard_map/fields/pallas_call | solution.py:372
  46.3 15.4 %maps.1 = bf16[16,128,4096]{2,1,0:T(8,128)(2,1)} custom-call(s32[256]{0:T(256)S(1)} %copy-done.2, bf16[256,32,128]{2,1,0:T(8,128)(2,1)S(1)} %fields.1.f_ref), custom_call_target="tpu_custom_call" | custom-call | tf_op jit(solution)/shard_map/maps/pallas_call | solution.py:351
Async XLA Ops:
  0.8 1.0 %copy-start = (f32[2,16,32,128]{3,2,1,0:T(8,128)S(1)}, f32[2,16,32,128]{3,2,1,0:T(8,128)}, u32[]{:S(2)}) copy-start(f32[2,16,32,128]{3,2,1,0:T(8,128)} %param.5) | copy-start | bytes 1572868
  1.8 0.7 %copy-start.1 = (s32[2048]{0:T(1024)S(1)}, s32[2048]{0:T(1024)}, u32[]{:S(2)}) copy-start(s32[2048]{0:T(1024)} %param.7) | copy-start | bytes 24580
  2.5 0.7 %copy-start.2 = (s32[256]{0:T(256)S(1)}, s32[256]{0:T(256)}, u32[]{:S(2)}) copy-start(s32[256]{0:T(256)} %mode_ref.3) | copy-start | bytes 3076

commit v3 on v2

v3 whole, which is shorter than its diff:
```python
import math

import jax
import jax.numpy as jnp
import numpy as np
from jax import lax
from jax.experimental import pallas as pl
from jax.experimental.pallas import tpu as pltpu
from jax.sharding import PartitionSpec as P

L = 256
M = 256
NSIDE = 1024
NPHI = 4096
ROWS = 128
SH = 16
LB = 64
GROUP = 8
KL = L // GROUP
SLOTS = 16
HALF = SLOTS // 2
WAVES = 128
MESH = pl.DeviceIdType.MESH


def start_norms():
    value = [
        0.5 * (math.log((2 * k + 1) / (4 * math.pi)) + math.lgamma(k + 0.5) - math.lgamma(0.5) - math.lgamma(k + 1.0))
        for k in range(M)
    ]
    table = np.zeros((M, ROWS), np.float32)
    table[:, 0] = value
    return table


def legendre_block(block, log_height, slope, norm_ref, table_ref):
    base = block * LB
    degree = base + lax.broadcasted_iota(jnp.int32, (LB, ROWS), 0)
    degree_f = degree.astype(jnp.float32)
    square = degree_f * (degree_f + 1.0)
    start = jnp.exp(norm_ref[base:base + LB, 0:1] + 0.5 * degree_f * log_height)
    unroll = 8

    def clear(i, _):
        for u in range(unroll):
            table_ref[base + LB + i * unroll + u, base:base + LB, :] = jnp.zeros((LB, ROWS), jnp.bfloat16)
        return 0

    lax.fori_loop(0, (M - LB - base) // unroll, clear, 0)

    def descend(first, count, carry, starting):
        def steps(i, carry):
            p, above, root = carry
            for u in range(unroll):
                m = first - 1 - (i * unroll + u)
                upper = (m + 1).astype(jnp.float32)
                e = square - upper * (upper - 1.0)
                inv = lax.rsqrt(jnp.maximum(e, 1.0) if starting else e)
                value = inv * ((upper * slope) * p - root * above)
                if starting:
                    value = jnp.where(degree == m, start, value)
                table_ref[m, base:base + LB, :] = value.astype(jnp.bfloat16)
                above, p, root = p, value, e * inv
            return p, above, root

        return lax.fori_loop(0, count // unroll, steps, carry)

    zero = jnp.zeros((LB, ROWS), jnp.float32)
    carry = descend(base + LB, LB, (zero, zero, zero), True)
    if base:
        descend(base, base, carry, False)


def turn_tables(cycles, cos_ref, sin_ref):
    odd = (lax.rem(cycles + 1, 2) == 1)
    order = lax.broadcasted_iota(jnp.int32, (M, ROWS), 0).astype(jnp.float32)
    a = order * (math.pi / NPHI)
    q = a * a
    cosine = 1.0 - q * (0.5 - q * (1.0 / 24 - q * (1.0 / 720)))
    sine = a * (1.0 - q * (1.0 / 6 - q * (1.0 / 120 - q * (1.0 / 5040))))
    cos_ref[...] = jnp.where(odd, cosine, 1.0)
    sin_ref[...] = jnp.where(odd, sine, 0.0)


def field_of(order, coeffs, table_ref, cos_ref, sin_ref):
    f = jnp.dot(coeffs, table_ref[order], preferred_element_type=jnp.float32)
    c = cos_ref[pl.ds(order, 1), :]
    s = sin_ref[pl.ds(order, 1), :]
    fr, fi = f[:SH], f[SH:]
    return (fr * c - fi * s).astype(jnp.bfloat16), (fr * s + fi * c).astype(jnp.bfloat16)


def radial(cot_ref, bes_ref, stage_ref, send_ref):
    def degree(k, _):
        for u in range(8):
            l = k * 8 + u
            c = cot_ref[pl.ds(l, 2 * SLOTS, stride=KL), :].astype(jnp.bfloat16)
            w = bes_ref[pl.ds(pl.multiple_of(l * WAVES, WAVES), WAVES), :].astype(jnp.bfloat16)
            stage_ref[pl.ds(l, 2 * SLOTS, stride=KL), :] = jnp.dot(c, w, preferred_element_type=jnp.float32)
        return 0

    lax.fori_loop(0, KL // 8, degree, 0)
    for q in range(8):
        tile = stage_ref[q * 128:(q + 1) * 128, :].T.astype(jnp.bfloat16)
        for h in range(GROUP):
            send_ref[h, q] = tile[h * SH:(h + 1) * SH]


def shuffle_matrix(perm_ref):
    k = lax.broadcasted_iota(jnp.int32, (512, 512), 0)
    n = lax.broadcasted_iota(jnp.int32, (512, 512), 1)
    to = ((k & 96) << 2) | ((k & 384) >> 2) | (k & 31)
    perm_ref[...] = jnp.where(to == n, 1.0, 0.0).astype(jnp.bfloat16)


def twiddles(tab_ref):
    half = M // 2
    rows = 32

    def part(index, _):
        par, first = lax.rem(index, 2), index // 2 * rows
        lane = lax.broadcasted_iota(jnp.int32, (rows, 128), 1)
        m = 2 * (first + lax.broadcasted_iota(jnp.int32, (rows, 128), 0)) + par
        a = m.astype(jnp.float32) * (2.0 * math.pi / NPHI)
        q = a * a
        tc = 1.0 - q * (0.5 - q * (1.0 / 24 - q * (1.0 / 720 - q * (1.0 / 40320))))
        ts = a * (1.0 - q * (1.0 / 6 - q * (1.0 / 120 - q * (1.0 / 5040 - q * (1.0 / 362880)))))
        c, s = jnp.where(m == 0, 2.0 / L, 4.0 / L), jnp.zeros((rows, 128), jnp.float32)
        for b in range(7):
            on = (lane & (1 << b)) != 0
            c, s = jnp.where(on, c * tc - s * ts, c), jnp.where(on, s * tc + c * ts, s)
            tc, ts = tc * tc - ts * ts, 2.0 * tc * ts
        top = pl.multiple_of(first, rows)
        for j in range(NPHI // 2 // 128):
            tab_ref[par, pl.ds(top, rows), j * 128:(j + 1) * 128] = c.astype(jnp.bfloat16)
            tab_ref[par, pl.ds(half + top, rows), j * 128:(j + 1) * 128] = (-s).astype(jnp.bfloat16)
            c, s = c * tc - s * ts, s * tc + c * ts
        return 0

    lax.fori_loop(0, 2 * half // rows, part, 0)


def inverse_order(mode_ref, inv_ref):
    order = lax.broadcasted_iota(jnp.int32, (M, M), 0)
    hit = jnp.where(mode_ref[...] == order, 1.0, 0.0).astype(jnp.bfloat16)
    slot = lax.broadcasted_iota(jnp.int32, (8, M), 1).astype(jnp.float32).astype(jnp.bfloat16)
    found = lax.dot_general(slot, hit, (((1,), (1,)), ((), ())), preferred_element_type=jnp.float32)
    inv_ref[...] = found[:1].astype(jnp.int32)


def relayout(recv_ref, perm_ref, own, block_ref):
    for h in range(2):
        x = jnp.concatenate([recv_ref[4 * h + j].reshape(128, 128) for j in range(4)], axis=1)
        y = jnp.dot(x, perm_ref[...], preferred_element_type=jnp.float32).astype(jnp.bfloat16)
        for q in range(8):
            for i in range(4):
                c, t = divmod(4 * q + i, SLOTS)
                block_ref[own, t, c * SH:(c + 1) * SH, h * 128:(h + 1) * 128] = y[q * SH:(q + 1) * SH, i * 128:(i + 1) * 128]


def fields_kernel(
    mode_hbm, order_hbm, cyc_hbm, norm_hbm, cot_hbm, bes_hbm, out_ref, tab_ref, inv_ref,
    mode_ref, order_ref, cyc_ref, norm_ref, table_ref, cos_ref, sin_ref,
    cot_ref, bes_ref, rad_ref, send_ref, recv_ref, perm_ref, block_ref,
    load_sem, a2a_send, a2a_recv, ring_send, ring_recv,
):
    own = lax.axis_index("blk")
    shell = lax.axis_index("shell")
    core = lax.rem(own, 2)
    x = lax.rem(own // 2, 4)
    z = own // 8
    d = 1 - 2 * core

    def at(dz, k):
        return lax.rem(z + dz, 2) * 8 + lax.rem(x + k * d + 8, 4) * 2 + core

    ahead, behind, across, sibling = at(0, 1), at(0, -1), at(1, 0), own + d

    pairs = [
        (cot_hbm, cot_ref), (bes_hbm, bes_ref), (cyc_hbm, cyc_ref), (norm_hbm, norm_ref), (mode_hbm, mode_ref), (order_hbm, order_ref)
    ]
    loads = [pltpu.make_async_copy(a, b, load_sem.at[i]) for i, (a, b) in enumerate(pairs)]
    for copy in loads:
        copy.start()
    barrier = pltpu.get_barrier_semaphore()
    for peer in (ahead, behind, across, sibling):
        pl.semaphore_signal(barrier, inc=1, device_id={"blk": peer}, device_id_type=MESH)
    for k in range(1, GROUP):
        pl.semaphore_signal(barrier, inc=1, device_id={"shell": lax.rem(shell + k, GROUP)}, device_id_type=MESH)

    for copy in loads[:2]:
        copy.wait()
    radial(cot_ref, bes_ref, rad_ref, send_ref)
    pl.semaphore_wait(barrier, 4 + GROUP - 1)
    exchange = []
    for k in range(1, GROUP):
        to = lax.rem(shell + k, GROUP)
        copy = pltpu.make_async_remote_copy(
            src_ref=send_ref.at[to], dst_ref=recv_ref.at[shell], send_sem=a2a_send.at[k - 1], recv_sem=a2a_recv.at[k - 1],
            device_id={"shell": to}, device_id_type=MESH,
        )
        copy.start()
        exchange.append(copy)
    recv_ref[shell] = send_ref[shell]
    shuffle_matrix(perm_ref)
    for copy in loads[2:]:
        copy.wait()
    cycles = cyc_ref[pl.ds(own, 1), :]
    height = (2.0 * NSIDE - 2.0 * cycles.astype(jnp.float32)) / (3.0 * NSIDE)
    width = 1.0 - height * height
    log_height, slope = jnp.log(width), 2.0 * height * lax.rsqrt(width)
    turn_tables(cycles, cos_ref, sin_ref)
    twiddles(tab_ref)

    def table(block):
        legendre_block(block, log_height, slope, norm_ref, table_ref)

    table(0)
    for k in range(1, GROUP):
        source = lax.rem(shell - k + GROUP, GROUP)
        pltpu.make_async_remote_copy(
            src_ref=send_ref.at[source], dst_ref=recv_ref.at[source], send_sem=a2a_send.at[k - 1], recv_sem=a2a_recv.at[k - 1],
            device_id={"shell": source}, device_id_type=MESH,
        ).wait_recv()
    relayout(recv_ref, perm_ref, own, block_ref)

    sent = []

    def piece(part, index):
        return block_ref.at[index, pl.ds(HALF * part, HALF)]

    def describe(part, index, to, slot):
        return pltpu.make_async_remote_copy(
            src_ref=piece(part, index), dst_ref=piece(part, index), send_sem=ring_send.at[slot],
            recv_sem=ring_recv.at[part, index], device_id={"blk": to}, device_id_type=MESH,
        )

    def send(part, index, *targets):
        for to in targets:
            copy = describe(part, index, to, len(sent))
            copy.start()
            sent.append(copy)

    def arrive(part, index):
        describe(part, index, sibling, 0).wait_recv()

    def slots(*pieces):
        def step(k, _):
            for u in range(4):
                for part, index in pieces:
                    t = HALF * part + k * 4 + u
                    g = index * SLOTS + t
                    re, im = field_of(mode_ref[g], block_ref[index, t], table_ref, cos_ref, sin_ref)
                    out_ref[g, :SH, :] = re
                    out_ref[g, SH:, :] = im
            return 0

        lax.fori_loop(0, HALF // 4, step, 0)

    def both(*pieces):
        other = [(part, index + d) for part, index in pieces]
        for part, index in other:
            arrive(part, index)
        slots(*pieces, *other)

    for part in range(2):
        send(part, own, across, ahead, behind)
    for part in range(2):
        send(part, own, sibling)
    table(3)
    arrive(0, at(1, 0))
    send(0, at(1, 0), ahead, behind)
    arrive(0, at(0, -1))
    send(0, at(0, -1), ahead)
    arrive(0, at(0, 1))
    for index in (at(1, 0), at(0, -1), at(0, 1)):
        send(0, index, sibling)
    table(2)
    arrive(1, at(0, -1))
    send(1, at(0, -1), ahead, across)
    arrive(1, at(0, 1))
    send(1, at(0, 1), across)
    for index in (at(0, -1), at(0, 1)):
        send(1, index, sibling)
    table(1)
    inverse_order(order_ref, inv_ref)
    arrive(0, at(1, -1))
    send(0, at(1, -1), ahead)
    arrive(1, at(0, 2))
    send(1, at(0, 2), across)
    arrive(0, at(0, 2))
    arrive(0, at(1, 1))
    for part, index in ((0, at(1, -1)), (1, at(0, 2)), (0, at(0, 2)), (0, at(1, 1))):
        send(part, index, sibling)
    both((0, own), (1, own))
    both((0, at(1, 0)), (0, at(0, -1)))
    both((0, at(0, 1)), (1, at(0, -1)))
    for index in (at(1, 0), at(1, -1), at(1, 1)):
        arrive(1, index)
        send(1, index, sibling)
    both((1, at(0, 1)), (0, at(1, -1)))
    both((1, at(0, 2)), (0, at(0, 2)))
    arrive(0, at(1, 2))
    send(0, at(1, 2), sibling)
    arrive(1, at(1, 2))
    send(1, at(1, 2), sibling)
    both((0, at(1, 1)), (1, at(1, 0)))
    both((1, at(1, -1)), (1, at(1, 1)))
    both((0, at(1, 2)), (1, at(1, 2)))
    for copy in exchange + sent:
        copy.wait_send()


SPS = 2
JC = 512


def maps_kernel(inv_ref, f_ref, tab_ref, out_ref, g_ref, even_ref, odd_ref):
    half = M // 2
    step = pl.program_id(0)
    last = pl.num_programs(0) - 1

    def sorted_rows(k, _):
        for par in range(2):
            f = jnp.stack([f_ref[inv_ref[0, 32 * k + 2 * u + par]] for u in range(16)])
            for c in range(2):
                w = jnp.transpose(f[:, c * SH:(c + 1) * SH], (1, 0, 2))
                row = pl.multiple_of(par * M + c * half + k * 16, 16)
                for s in range(SH):
                    g_ref[s, pl.ds(row, 16), :] = w[s]
        return 0

    def prepare(first, slot):
        for i in range(SPS):
            even_ref[slot, i * ROWS:(i + 1) * ROWS, :] = g_ref[first + i, :M, :].T
            odd_ref[slot, i * ROWS:(i + 1) * ROWS, :] = g_ref[first + i, M:, :].T

    @pl.when(step == 0)
    def _():
        lax.fori_loop(0, M // 32, sorted_rows, 0)
        prepare(0, 0)

    slot = lax.rem(step, 2)
    even, odd = even_ref[slot], odd_ref[slot]
    prepare(jnp.minimum(step + 1, last) * SPS, 1 - slot)
    for j in range(0, NPHI // 2, JC):
        e = jnp.dot(even, tab_ref[0, :, j:j + JC], preferred_element_type=jnp.float32)
        o = jnp.dot(odd, tab_ref[1, :, j:j + JC], preferred_element_type=jnp.float32)
        p = (e + o).astype(jnp.bfloat16)
        q = (e - o).astype(jnp.bfloat16)
        for i in range(SPS):
            out_ref[i, :, j:j + JC] = p[i * ROWS:(i + 1) * ROWS]
            out_ref[i, :, NPHI // 2 + j:NPHI // 2 + j + JC] = q[i * ROWS:(i + 1) * ROWS]


def maps_call(inverse, fields, table):
    return pl.pallas_call(
        maps_kernel,
        out_shape=jax.ShapeDtypeStruct((SH, ROWS, NPHI), jnp.bfloat16),
        grid=(SH // SPS,),
        in_specs=[
            pl.BlockSpec(memory_space=pltpu.SMEM),
            pl.BlockSpec(memory_space=pltpu.VMEM),
            pl.BlockSpec(memory_space=pltpu.VMEM),
        ],
        out_specs=pl.BlockSpec((SPS, ROWS, NPHI), lambda i: (i, 0, 0)),
        scratch_shapes=[
            pltpu.VMEM((SH, 2 * M, ROWS), jnp.bfloat16),
            pltpu.VMEM((2, SPS * ROWS, M), jnp.bfloat16),
            pltpu.VMEM((2, SPS * ROWS, M), jnp.bfloat16),
        ],
        compiler_params=pltpu.CompilerParams(vmem_limit_bytes=40 << 20),
        name="maps",
    )(inverse, fields, table)


def fields_call(cotangent, bessel, cycle_index, mode_order):
    vmem = pl.BlockSpec(memory_space=pltpu.VMEM)
    hbm = pl.BlockSpec(memory_space=pltpu.HBM)
    return pl.pallas_call(
        fields_kernel,
        out_shape=(
            jax.ShapeDtypeStruct((M, 2 * SH, ROWS), jnp.bfloat16),
            jax.ShapeDtypeStruct((2, M, NPHI // 2), jnp.bfloat16),
            jax.ShapeDtypeStruct((1, M), jnp.int32),
        ),
        in_specs=[hbm] * 6,
        out_specs=(vmem, vmem, vmem),
        scratch_shapes=[
            pltpu.SMEM((M,), jnp.int32),
            pltpu.VMEM((1, M), jnp.int32),
            pltpu.VMEM((16, ROWS), jnp.int32),
            pltpu.VMEM((M, ROWS), jnp.float32),
            pltpu.VMEM((M, L, ROWS), jnp.bfloat16),
            pltpu.VMEM((M, ROWS), jnp.float32),
            pltpu.VMEM((M, ROWS), jnp.float32),
            pltpu.VMEM((2 * SLOTS * KL, WAVES), jnp.float32),
            pltpu.VMEM((KL * WAVES, 128), jnp.float32),
            pltpu.VMEM((2 * SLOTS * KL, 128), jnp.float32),
            pltpu.VMEM((GROUP, 8, SH, 128), jnp.bfloat16),
            pltpu.VMEM((GROUP, 8, SH, 128), jnp.bfloat16),
            pltpu.VMEM((512, 512), jnp.bfloat16),
            pltpu.VMEM((16, SLOTS, 2 * SH, L), jnp.bfloat16),
            pltpu.SemaphoreType.DMA((6,)),
            pltpu.SemaphoreType.DMA((GROUP - 1,)),
            pltpu.SemaphoreType.DMA((GROUP - 1,)),
            pltpu.SemaphoreType.DMA((30,)),
            pltpu.SemaphoreType.DMA((2, 16)),
        ],
        compiler_params=pltpu.CompilerParams(vmem_limit_bytes=48 << 20, collective_id=0, has_side_effects=True),
        name="fields",
    )(
        mode_order, mode_order.reshape(1, -1), cycle_index.reshape(-1, ROWS), jnp.asarray(start_norms()),
        cotangent.reshape(-1, WAVES), bessel.reshape(-1, 128),
    )


def per_device(cotangent, bessel, cycle_index, mode_order):
    fields, table, inverse = fields_call(cotangent, bessel, cycle_index, mode_order)
    return maps_call(inverse, fields, table)


def solution(mesh):
    return jax.shard_map(
        per_device,
        mesh=mesh,
        in_specs=(P(None, "blk", "shell", None), P("shell", None, None), P(), P()),
        out_specs=P("shell", "blk", None),
        check_vma=False,
    )
```

time: 62.3 us -> 48.4 us (0.78)
  Pallas kernels: 58.5 us -> 44.9 us
    pallas_call x1, Pallas kernels: 43.1 us -> 34.2 us  [fields_call(): pl.pallas_call(fields_kernel, out_shape=(jax.ShapeDtypeStruct((M, 2 * SH,...]
    pallas_call x1, Pallas kernels: 15.4 us -> 10.6 us  [maps_call(): pl.pallas_call(maps_kernel, out_shape=jax.ShapeDtypeStruct((SH, ROWS, NPH...]
    unnamed x6 -> x8, local copies, waits for them, and re-layouts: 2.41 us -> 3.32 us
    another operation x1 -> x0, local copies, waits for them, and re-layouts: 0.77 us -> none
where the time goes in v3:
time: 48.4 us; the launch traced here: 48.2 us
  Pallas kernels  44.9 us (93%)
  local copies, waits for them, and re-layouts  3.32 us (7%)
    pallas_call x1, Pallas kernels, fields_call(): pl.pallas_call(fields_kernel, out_shape=(jax.ShapeDtypeStruct((M, 2 * SH,...  34.2 us
    pallas_call x1, Pallas kernels, maps_call(): pl.pallas_call(maps_kernel, out_shape=jax.ShapeDtypeStruct((SH, ROWS, NPH...  10.6 us
    unnamed x8, local copies, waits for them, and re-layouts  3.32 us

profile of v3, /device:TPU:1, one launch (start us, length us, event | category | flops | bytes accessed | tf_op | source)
XLA Modules:
  0.0 48.2 jit_solution(8095110537682697712)
XLA Ops:
  0.0 0.0 copy-start
  0.0 1.0 %copy-done = f32[2,16,32,128]{3,2,1,0:T(8,128)S(1)} copy-done((f32[2,16,32,128]{3,2,1,0:T(8,128)S(1)}, f32[2,16,32,128]{3,2,1,0:T(8,128)}, u32[]{:S(2)}) %copy-start) | copy-done | bytes 524312
  1.0 0.0 copy-start.1
  1.0 0.9 %copy-done.1 = f32[256,128]{1,0:T(8,128)S(1)} copy-done((f32[256,128]{1,0:T(8,128)S(1)}, f32[256,128]{1,0:T(8,128)}, u32[]{:S(2)}) %copy-start.1) | copy-done | bytes 131096
  1.9 0.0 copy-start.2
  1.9 0.7 %copy-done.2 = s32[2048]{0:T(1024)S(1)} copy-done((s32[2048]{0:T(1024)S(1)}, s32[2048]{0:T(1024)}, u32[]{:S(2)}) %copy-start.2) | copy-done | bytes 8216
  2.6 0.0 copy-start.3
  2.6 0.7 %copy-done.3 = s32[256]{0:T(256)S(1)} copy-done((s32[256]{0:T(256)S(1)}, s32[256]{0:T(256)}, u32[]{:S(2)}) %copy-start.3) | copy-done | bytes 1048
  3.3 34.2 %fields.1 = (bf16[256,32,128]{2,1,0:T(8,128)(2,1)S(1)}, bf16[2,256,2048]{2,1,0:T(8,128)(2,1)S(1)}, s32[1,256]{1,0:T(1,128)S(1)}) custom-call(s32[256]{0:T(256)S(1)} %copy-done.3, s32[1,256]{1,0:T(1,128)S(1)} %bitcast.6, s32[16,128]{1,0:T(8,128)S(1)} %bitcast.5, f32[256,128]{1,0:T(8,128)S(1)} %copy-done.1, f32[1024,128]{1,0:T(8,128)S(1)} %bitcast.4, ...), custom_call_target="tpu_custom_call" | custom-call | tf_op jit(solution)/shard_map/fields/pallas_call | solution.py:380
  37.6 10.6 %maps.1 = bf16[16,128,4096]{2,1,0:T(8,128)(2,1)} custom-call(s32[1,256]{1,0:T(1,128)S(1)} %get-tuple-element.8.inv_ref, bf16[256,32,128]{2,1,0:T(8,128)(2,1)S(1)} %get-tuple-element.9.f_ref, bf16[2,256,2048]{2,1,0:T(8,128)(2,1)S(1)} %get-tuple-element.10.tab_ref), custom_call_target="tpu_custom_call" | custom-call | tf_op jit(solution)/shard_map/maps/pallas_call | solution.py:357
Async XLA Ops:
  0.0 1.0 %copy-start = (f32[2,16,32,128]{3,2,1,0:T(8,128)S(1)}, f32[2,16,32,128]{3,2,1,0:T(8,128)}, u32[]{:S(2)}) copy-start(f32[2,16,32,128]{3,2,1,0:T(8,128)} %param.5) | copy-start | bytes 1572868
  1.0 0.9 %copy-start.1 = (f32[256,128]{1,0:T(8,128)S(1)}, f32[256,128]{1,0:T(8,128)}, u32[]{:S(2)}) copy-start(f32[256,128]{1,0:T(8,128)} %constant.2.clone.norm_hbm) | copy-start | bytes 393220
  1.9 0.7 %copy-start.2 = (s32[2048]{0:T(1024)S(1)}, s32[2048]{0:T(1024)}, u32[]{:S(2)}) copy-start(s32[2048]{0:T(1024)} %param.7) | copy-start | bytes 24580
  2.6 0.7 %copy-start.3 = (s32[256]{0:T(256)S(1)}, s32[256]{0:T(256)}, u32[]{:S(2)}) copy-start(s32[256]{0:T(256)} %mode_hbm.1) | copy-start | bytes 3076

commit v4 on v3

v4 whole, which is shorter than its diff:
```python
import math

import jax
import jax.numpy as jnp
import numpy as np
from jax import lax
from jax.experimental import pallas as pl
from jax.experimental.pallas import tpu as pltpu
from jax.sharding import PartitionSpec as P

L = 256
M = 256
NSIDE = 1024
NPHI = 4096
ROWS = 128
SH = 16
LB = 64
GROUP = 8
KL = L // GROUP
SLOTS = 16
HALF = SLOTS // 2
WAVES = 128
MESH = pl.DeviceIdType.MESH


def scaled_norms():
    log_gamma = np.array([0.0, 0.0] + [math.lgamma(k) for k in range(2, 2 * L + 1)])
    m, l = np.arange(M)[:, None], np.arange(L)[None, :]
    top = l // LB * LB + LB - 1
    low = np.minimum(m, l)
    log_gain = 0.5 * (
        (l - low) * np.log(top * (top + 1.0)) + log_gamma[l + low + 1] - log_gamma[2 * l + 1] - log_gamma[l - low + 1]
    )
    middle = 0.5 * log_gain[0]
    gain = np.where(m <= l, np.exp(log_gain - middle), 0.0).astype(np.float32)
    start = np.zeros((L, ROWS), np.float32)
    for k in range(L):
        norm = math.log((2 * k + 1) / (4 * math.pi)) + math.lgamma(k + 0.5) - math.lgamma(0.5) - math.lgamma(k + 1.0)
        start[k, 0] = 0.5 * norm + middle[k]
    return start, np.concatenate([gain[:, :ROWS], gain[:, ROWS:]])


def twiddles():
    tables = []
    for parity in range(2):
        m = np.arange(parity, M, 2)[:, None]
        angle = m * np.arange(NPHI // 2)[None, :] % NPHI * (2.0 * math.pi / NPHI)
        w = np.where(m == 0, 2.0 / L, 4.0 / L)
        tables.append(np.concatenate([w * np.cos(angle), -w * np.sin(angle)]))
    return np.stack(tables).astype(np.float32)


def legendre_block(block, log_height, slope, start_ref, table_ref):
    base = block * LB
    groups = LB // 8
    top = base + LB - 1
    c = 1.0 / (top * (top + 1.0))
    sub = lax.broadcasted_iota(jnp.int32, (8, ROWS), 0)
    degrees = [base + 8 * g + sub for g in range(groups)]
    degree_f = [k.astype(jnp.float32) for k in degrees]
    square = [k * (k + 1.0) * c for k in degree_f]
    start = [
        jnp.exp(start_ref[base + 8 * g:base + 8 * g + 8, 0:1] + 0.5 * degree_f[g] * log_height) for g in range(groups)
    ]
    slope = slope * math.sqrt(c)
    unroll = 16

    def clear(i, _):
        for u in range(unroll):
            table_ref[base + LB + i * unroll + u, base:base + LB, :] = jnp.zeros((LB, ROWS), jnp.bfloat16)
        return 0

    lax.fori_loop(0, (M - LB - base) // unroll, clear, 0)

    def descend(first, count, carry, starting):
        def steps(i, carry):
            p, above = carry
            for u in range(unroll):
                m = first - 1 - (i * unroll + u)
                upper = (m + 1).astype(jnp.float32)
                lower = upper * (upper + 1.0) * c
                turn = slope * upper
                new = []
                for g in range(groups):
                    value = turn * p[g] - (square[g] - lower) * above[g]
                    if starting:
                        value = jnp.where(degrees[g] == m, start[g], value)
                    new.append(value)
                for g in range(0, groups, 2):
                    rows = jnp.concatenate([new[g], new[g + 1]], axis=0)
                    table_ref[m, base + 8 * g:base + 8 * g + 16, :] = rows.astype(jnp.bfloat16)
                p, above = new, p
            return p, above

        return lax.fori_loop(0, count // unroll, steps, carry)

    zero = [jnp.zeros((8, ROWS), jnp.float32)] * groups
    carry = descend(base + LB, LB, (zero, zero), True)
    if base:
        descend(base, base, carry, False)


def turn_tables(cycles, cos_ref, sin_ref):
    odd = (lax.rem(cycles + 1, 2) == 1)
    order = lax.broadcasted_iota(jnp.int32, (M, ROWS), 0).astype(jnp.float32)
    a = order * (math.pi / NPHI)
    q = a * a
    cosine = 1.0 - q * (0.5 - q * (1.0 / 24 - q * (1.0 / 720)))
    sine = a * (1.0 - q * (1.0 / 6 - q * (1.0 / 120 - q * (1.0 / 5040))))
    cos_ref[...] = jnp.where(odd, cosine, 1.0)
    sin_ref[...] = jnp.where(odd, sine, 0.0)


def field_of(order, coeffs, table_ref, cos_ref, sin_ref):
    f = jnp.dot(coeffs, table_ref[order], preferred_element_type=jnp.float32)
    c = cos_ref[pl.ds(order, 1), :]
    s = sin_ref[pl.ds(order, 1), :]
    fr, fi = f[:SH], f[SH:]
    return (fr * c - fi * s).astype(jnp.bfloat16), (fr * s + fi * c).astype(jnp.bfloat16)


def radial(group, cot_ref, bes_ref, stage_ref):
    for u in range(8):
        l = group * 8 + u
        c = cot_ref[pl.ds(l, 2 * SLOTS, stride=KL), :].astype(jnp.bfloat16)
        w = bes_ref[l * WAVES:(l + 1) * WAVES, :].astype(jnp.bfloat16)
        stage_ref[pl.ds(l, 2 * SLOTS, stride=KL), :] = jnp.dot(c, w, preferred_element_type=jnp.float32)


def arrange(part, stage_ref, send_ref):
    for n in range(4):
        q = n // 2 * 4 + 2 * part + n % 2
        tile = stage_ref[q * 128:(q + 1) * 128, :].T.astype(jnp.bfloat16)
        for h in range(GROUP):
            send_ref[part, h, n] = tile[h * SH:(h + 1) * SH]


def shuffle_matrix(perm_ref):
    k = lax.broadcasted_iota(jnp.int32, (512, 512), 0)
    n = lax.broadcasted_iota(jnp.int32, (512, 512), 1)
    to = ((k & 96) << 2) | ((k & 384) >> 2) | (k & 31)
    perm_ref[...] = jnp.where(to == n, 1.0, 0.0).astype(jnp.bfloat16)


def inverse_order(mode_ref, inv_ref):
    order = lax.broadcasted_iota(jnp.int32, (M, M), 0)
    hit = jnp.where(mode_ref[...] == order, 1.0, 0.0).astype(jnp.bfloat16)
    slot = lax.broadcasted_iota(jnp.int32, (8, M), 1).astype(jnp.float32).astype(jnp.bfloat16)
    found = lax.dot_general(slot, hit, (((1,), (1,)), ((), ())), preferred_element_type=jnp.float32)
    inv_ref[...] = found[:1].astype(jnp.int32)


def relayout(part, recv_ref, perm_ref, mode_ref, gain_ref, own, block_ref):
    for h in range(2):
        x = jnp.concatenate([recv_ref[part, 4 * h + j].reshape(64, 128) for j in range(4)], axis=1)
        y = jnp.dot(x, perm_ref[...], preferred_element_type=jnp.float32)
        for n in range(4):
            for i in range(4):
                c, t = n // 2, HALF * part + n % 2 * 4 + i
                gain = gain_ref[pl.ds(h * M + mode_ref[own * SLOTS + t], 1), :]
                block = y[n * SH:(n + 1) * SH, i * 128:(i + 1) * 128] * gain
                block_ref[own, t, c * SH:(c + 1) * SH, h * 128:(h + 1) * 128] = block.astype(jnp.bfloat16)


def fields_kernel(
    mode_hbm, order_hbm, cyc_hbm, start_hbm, gain_hbm, wave_hbm, cot_hbm, bes_hbm, out_ref, tab_ref, inv_ref,
    mode_ref, order_ref, cyc_ref, start_ref, gain_ref, table_ref, cos_ref, sin_ref,
    cot_ref, bes_ref, rad_ref, send_ref, recv_ref, perm_ref, block_ref,
    load_sem, a2a_send, a2a_recv, ring_send, ring_recv,
):
    own = lax.axis_index("blk")
    shell = lax.axis_index("shell")
    core = lax.rem(own, 2)
    x = lax.rem(own // 2, 4)
    z = own // 8
    d = 1 - 2 * core

    def at(dz, k):
        return lax.rem(z + dz, 2) * 8 + lax.rem(x + k * d + 8, 4) * 2 + core

    ahead, behind, across, sibling = at(0, 1), at(0, -1), at(1, 0), own + d

    quarter = KL * WAVES // 4
    pairs = [(cot_hbm, cot_ref)]
    pairs += [(bes_hbm.at[pl.ds(k * quarter, quarter)], bes_ref.at[pl.ds(k * quarter, quarter)]) for k in range(4)]
    pairs += [(cyc_hbm, cyc_ref), (start_hbm, start_ref), (mode_hbm, mode_ref), (order_hbm, order_ref), (gain_hbm, gain_ref)]
    pairs += [(wave_hbm, tab_ref)]
    loads = [pltpu.make_async_copy(a, b, load_sem.at[i]) for i, (a, b) in enumerate(pairs)]
    for copy in loads:
        copy.start()
    barrier = pltpu.get_barrier_semaphore()
    for peer in (ahead, behind, across, sibling):
        pl.semaphore_signal(barrier, inc=1, device_id={"blk": peer}, device_id_type=MESH)
    for k in range(1, GROUP):
        pl.semaphore_signal(barrier, inc=1, device_id={"shell": lax.rem(shell + k, GROUP)}, device_id_type=MESH)

    loads[0].wait()
    for k in range(4):
        loads[1 + k].wait()
        radial(k, cot_ref, bes_ref, rad_ref)
    exchange = []
    for part in range(2):
        arrange(part, rad_ref, send_ref)
        if part == 0:
            pl.semaphore_wait(barrier, 4 + GROUP - 1)
        for k in range(1, GROUP):
            to = lax.rem(shell + k, GROUP)
            copy = pltpu.make_async_remote_copy(
                src_ref=send_ref.at[part, to], dst_ref=recv_ref.at[part, shell],
                send_sem=a2a_send.at[part, k - 1], recv_sem=a2a_recv.at[part, k - 1],
                device_id={"shell": to}, device_id_type=MESH,
            )
            copy.start()
            exchange.append(copy)
        recv_ref[part, shell] = send_ref[part, shell]
    shuffle_matrix(perm_ref)
    for copy in loads[5:10]:
        copy.wait()
    cycles = jnp.broadcast_to(cyc_ref[pl.ds(own, 1), :], (8, ROWS))
    height = (2.0 * NSIDE - 2.0 * cycles.astype(jnp.float32)) / (3.0 * NSIDE)
    width = 1.0 - height * height
    log_height, slope = jnp.log(width), 2.0 * height * lax.rsqrt(width)
    turn_tables(cycles[:1], cos_ref, sin_ref)

    def table(block):
        legendre_block(block, log_height, slope, start_ref, table_ref)

    table(0)
    sent = []

    def piece(part, index):
        return block_ref.at[index, pl.ds(HALF * part, HALF)]

    def describe(part, index, to, slot):
        return pltpu.make_async_remote_copy(
            src_ref=piece(part, index), dst_ref=piece(part, index), send_sem=ring_send.at[slot],
            recv_sem=ring_recv.at[part, index], device_id={"blk": to}, device_id_type=MESH,
        )

    def send(part, index, *targets):
        for to in targets:
            copy = describe(part, index, to, len(sent))
            copy.start()
            sent.append(copy)

    def arrive(part, index):
        describe(part, index, sibling, 0).wait_recv()

    def slots(*pieces):
        def step(k, _):
            for u in range(4):
                for part, index in pieces:
                    t = HALF * part + k * 4 + u
                    g = index * SLOTS + t
                    re, im = field_of(mode_ref[g], block_ref[index, t], table_ref, cos_ref, sin_ref)
                    out_ref[g, :SH, :] = re
                    out_ref[g, SH:, :] = im
            return 0

        lax.fori_loop(0, HALF // 4, step, 0)

    def both(*pieces):
        other = [(part, index + d) for part, index in pieces]
        for part, index in other:
            arrive(part, index)
        slots(*pieces, *other)

    for part in range(2):
        for k in range(1, GROUP):
            source = lax.rem(shell - k + GROUP, GROUP)
            pltpu.make_async_remote_copy(
                src_ref=send_ref.at[part, source], dst_ref=recv_ref.at[part, source],
                send_sem=a2a_send.at[part, k - 1], recv_sem=a2a_recv.at[part, k - 1],
                device_id={"shell": source}, device_id_type=MESH,
            ).wait_recv()
        relayout(part, recv_ref, perm_ref, mode_ref, gain_ref, own, block_ref)
        send(part, own, across, ahead, behind)
    for part in range(2):
        send(part, own, sibling)
    table(3)
    arrive(0, at(1, 0))
    send(0, at(1, 0), ahead, behind)
    arrive(0, at(0, -1))
    send(0, at(0, -1), ahead)
    arrive(0, at(0, 1))
    for index in (at(1, 0), at(0, -1), at(0, 1)):
        send(0, index, sibling)
    table(2)
    arrive(1, at(0, -1))
    send(1, at(0, -1), ahead, across)
    arrive(1, at(0, 1))
    send(1, at(0, 1), across)
    for index in (at(0, -1), at(0, 1)):
        send(1, index, sibling)
    table(1)
    inverse_order(order_ref, inv_ref)
    arrive(0, at(1, -1))
    send(0, at(1, -1), ahead)
    arrive(1, at(0, 2))
    send(1, at(0, 2), across)
    arrive(0, at(0, 2))
    arrive(0, at(1, 1))
    for part, index in ((0, at(1, -1)), (1, at(0, 2)), (0, at(0, 2)), (0, at(1, 1))):
        send(part, index, sibling)
    both((0, own), (1, own))
    both((0, at(1, 0)), (0, at(0, -1)))
    both((0, at(0, 1)), (1, at(0, -1)))
    for index in (at(1, 0), at(1, -1), at(1, 1)):
        arrive(1, index)
        send(1, index, sibling)
    both((1, at(0, 1)), (0, at(1, -1)))
    both((1, at(0, 2)), (0, at(0, 2)))
    arrive(0, at(1, 2))
    send(0, at(1, 2), sibling)
    arrive(1, at(1, 2))
    send(1, at(1, 2), sibling)
    both((0, at(1, 1)), (1, at(1, 0)))
    both((1, at(1, -1)), (1, at(1, 1)))
    both((0, at(1, 2)), (1, at(1, 2)))
    for copy in exchange + sent:
        copy.wait_send()
    loads[10].wait()


GROUPS = (2, 4, 4, 4, 2)
JC = 1024


def maps_kernel(inv_ref, f_ref, tab_ref, out_hbm, g_ref, even_ref, odd_ref, map_ref, sem):
    half = M // 2
    firsts = [sum(GROUPS[:i]) for i in range(len(GROUPS))]

    def sorted_rows(k, _):
        for par in range(2):
            f = jnp.stack([f_ref[inv_ref[0, 32 * k + 2 * u + par]] for u in range(16)])
            for c in range(2):
                w = jnp.transpose(f[:, c * SH:(c + 1) * SH], (1, 0, 2))
                row = pl.multiple_of(par * M + c * half + k * 16, 16)
                for s in range(SH):
                    g_ref[s, pl.ds(row, 16), :] = w[s]
        return 0

    def prepare(group):
        for i in range(GROUPS[group]):
            even_ref[group % 2, i * ROWS:(i + 1) * ROWS, :] = g_ref[firsts[group] + i, :M, :].T
            odd_ref[group % 2, i * ROWS:(i + 1) * ROWS, :] = g_ref[firsts[group] + i, M:, :].T

    def copies(group):
        slot = group % 2
        return [
            pltpu.make_async_copy(map_ref.at[slot, i], out_hbm.at[firsts[group] + i], sem.at[slot, i])
            for i in range(GROUPS[group])
        ]

    lax.fori_loop(0, M // 32, sorted_rows, 0)
    prepare(0)
    for group, size in enumerate(GROUPS):
        slot = group % 2
        if group >= 2:
            for copy in copies(group - 2):
                copy.wait()
        if group + 1 < len(GROUPS):
            prepare(group + 1)

        def pixels(k, _):
            low = slice(k * JC, k * JC + JC)
            high = slice(NPHI // 2 + k * JC, NPHI // 2 + k * JC + JC)
            even, odd = even_ref[slot, :size * ROWS, :], odd_ref[slot, :size * ROWS, :]
            e = jnp.dot(even, tab_ref[0, :, low], preferred_element_type=jnp.float32)
            o = jnp.dot(odd, tab_ref[1, :, low], preferred_element_type=jnp.float32)
            map_ref[slot, :size, :, low] = (e + o).astype(jnp.bfloat16).reshape(size, ROWS, JC)
            map_ref[slot, :size, :, high] = (e - o).astype(jnp.bfloat16).reshape(size, ROWS, JC)
            return 0

        for k in range(NPHI // 2 // JC):
            pixels(k, 0)
        for copy in copies(group):
            copy.start()
    for group in range(len(GROUPS) - 2, len(GROUPS)):
        for copy in copies(group):
            copy.wait()


def maps_call(inverse, fields, table):
    most = max(GROUPS)
    return pl.pallas_call(
        maps_kernel,
        out_shape=jax.ShapeDtypeStruct((SH, ROWS, NPHI), jnp.bfloat16),
        in_specs=[
            pl.BlockSpec(memory_space=pltpu.SMEM),
            pl.BlockSpec(memory_space=pltpu.VMEM),
            pl.BlockSpec(memory_space=pltpu.VMEM),
        ],
        out_specs=pl.BlockSpec(memory_space=pl.ANY),
        scratch_shapes=[
            pltpu.VMEM((SH, 2 * M, ROWS), jnp.bfloat16),
            pltpu.VMEM((2, most * ROWS, M), jnp.bfloat16),
            pltpu.VMEM((2, most * ROWS, M), jnp.bfloat16),
            pltpu.VMEM((2, most, ROWS, NPHI), jnp.bfloat16),
            pltpu.SemaphoreType.DMA((2, most)),
        ],
        compiler_params=pltpu.CompilerParams(vmem_limit_bytes=40 << 20),
        name="maps",
    )(inverse, fields, table)


def fields_call(cotangent, bessel, cycle_index, mode_order):
    start, gain = scaled_norms()
    wave = jnp.asarray(twiddles().astype(jnp.bfloat16))
    vmem = pl.BlockSpec(memory_space=pltpu.VMEM)
    hbm = pl.BlockSpec(memory_space=pltpu.HBM)
    return pl.pallas_call(
        fields_kernel,
        out_shape=(
            jax.ShapeDtypeStruct((M, 2 * SH, ROWS), jnp.bfloat16),
            jax.ShapeDtypeStruct((2, M, NPHI // 2), jnp.bfloat16),
            jax.ShapeDtypeStruct((1, M), jnp.int32),
        ),
        in_specs=[hbm] * 8,
        out_specs=(vmem, vmem, vmem),
        scratch_shapes=[
            pltpu.SMEM((M,), jnp.int32),
            pltpu.VMEM((1, M), jnp.int32),
            pltpu.VMEM((16, ROWS), jnp.int32),
            pltpu.VMEM((L, ROWS), jnp.float32),
            pltpu.VMEM((2 * M, ROWS), jnp.float32),
            pltpu.VMEM((M, L, ROWS), jnp.bfloat16),
            pltpu.VMEM((M, ROWS), jnp.float32),
            pltpu.VMEM((M, ROWS), jnp.float32),
            pltpu.VMEM((2 * SLOTS * KL, WAVES), jnp.float32),
            pltpu.VMEM((KL * WAVES, 128), jnp.float32),
            pltpu.VMEM((2 * SLOTS * KL, 128), jnp.float32),
            pltpu.VMEM((2, GROUP, 4, SH, 128), jnp.bfloat16),
            pltpu.VMEM((2, GROUP, 4, SH, 128), jnp.bfloat16),
            pltpu.VMEM((512, 512), jnp.bfloat16),
            pltpu.VMEM((16, SLOTS, 2 * SH, L), jnp.bfloat16),
            pltpu.SemaphoreType.DMA((11,)),
            pltpu.SemaphoreType.DMA((2, GROUP - 1)),
            pltpu.SemaphoreType.DMA((2, GROUP - 1)),
            pltpu.SemaphoreType.DMA((30,)),
            pltpu.SemaphoreType.DMA((2, 16)),
        ],
        compiler_params=pltpu.CompilerParams(vmem_limit_bytes=48 << 20, collective_id=0, has_side_effects=True),
        name="fields",
    )(
        *(
            pltpu.with_memory_space_constraint(a, pltpu.HBM)
            for a in (
                mode_order, mode_order.reshape(1, -1), cycle_index.reshape(-1, ROWS),
                jnp.asarray(start), jnp.asarray(gain), wave,
                cotangent.reshape(-1, WAVES), bessel.reshape(-1, 128),
            )
        )
    )


def per_device(cotangent, bessel, cycle_index, mode_order):
    fields, table, inverse = fields_call(cotangent, bessel, cycle_index, mode_order)
    return maps_call(inverse, fields, table)


def solution(mesh):
    return jax.shard_map(
        per_device,
        mesh=mesh,
        in_specs=(P(None, "blk", "shell", None), P("shell", None, None), P(), P()),
        out_specs=P("shell", "blk", None),
        check_vma=False,
    )
```

time: 48.4 us -> 42.2 us (0.87)
  local copies, waits for them, and re-layouts: 3.32 us -> 0 us
  Pallas kernels: 44.9 us -> 42 us
    unnamed x8 -> x0, local copies, waits for them, and re-layouts: 3.32 us -> none
    pallas_call x1, Pallas kernels: 10.6 us -> 9.05 us  [maps_call(): pl.pallas_call(maps_kernel, out_shape=jax.ShapeDtypeStruct((SH, ROWS, NPH...]
    pallas_call x1, Pallas kernels: 34.2 us -> 33 us  [fields_call(): pl.pallas_call(fields_kernel, out_shape=(jax.ShapeDtypeStruct((M, 2 * SH,...]
where the time goes in v4:
time: 42.2 us; the launch traced here: 42.1 us
  Pallas kernels  42 us (100%)
    pallas_call x1, Pallas kernels, fields_call(): pl.pallas_call(fields_kernel, out_shape=(jax.ShapeDtypeStruct((M, 2 * SH,...  33 us
    pallas_call x1, Pallas kernels, maps_call(): pl.pallas_call(maps_kernel, out_shape=jax.ShapeDtypeStruct((SH, ROWS, NPH...  9.05 us

profile of v4, /device:TPU:1, one launch (start us, length us, event | category | flops | bytes accessed | tf_op | source)
XLA Modules:
  0.0 42.1 jit_solution(2459867524145945892)
XLA Ops:
  0.0 33.0 %fields.1 = (bf16[256,32,128]{2,1,0:T(8,128)(2,1)S(1)}, bf16[2,256,2048]{2,1,0:T(8,128)(2,1)S(1)}, s32[1,256]{1,0:T(1,128)S(1)}) custom-call(s32[256]{0:T(256)} %mode_hbm.1, s32[1,256]{1,0:T(1,128)} %bitcast.7, s32[16,128]{1,0:T(8,128)} %bitcast.6, f32[256,128]{1,0:T(8,128)} %constant.7.clone.start_hbm, f32[512,128]{1,0:T(8,128)} %constant.8.clone.gain_hbm, ...), custom_call_target="tpu_custom_call" | custom-call | tf_op jit(solution)/shard_map/fields/pallas_call | solution.py:412
  33.0 9.1 %maps.1 = bf16[16,128,4096]{2,1,0:T(8,128)(2,1)} custom-call(s32[1,256]{1,0:T(1,128)S(1)} %get-tuple-element.8.inv_ref, bf16[256,32,128]{2,1,0:T(8,128)(2,1)S(1)} %get-tuple-element.9.f_ref, bf16[2,256,2048]{2,1,0:T(8,128)(2,1)S(1)} %get-tuple-element.10.tab_ref), custom_call_target="tpu_custom_call" | custom-call | tf_op jit(solution)/shard_map/maps/pallas_call | solution.py:386

commit v5 on v4

--- a/solution.py
+++ b/solution.py
@@ -181,7 +181,7 @@
     ahead, behind, across, sibling = at(0, 1), at(0, -1), at(1, 0), own + d
 
     quarter = KL * WAVES // 4
-    pairs = [(cot_hbm, cot_ref)]
+    pairs = [(cot_hbm, cot_ref.at[pl.ds(0, 2 * SLOTS * KL)])]
     pairs += [(bes_hbm.at[pl.ds(k * quarter, quarter)], bes_ref.at[pl.ds(k * quarter, quarter)]) for k in range(4)]
     pairs += [(cyc_hbm, cyc_ref), (start_hbm, start_ref), (mode_hbm, mode_ref), (order_hbm, order_ref), (gain_hbm, gain_ref)]
     pairs += [(wave_hbm, tab_ref)]
@@ -427,9 +427,9 @@
             pltpu.VMEM((M, L, ROWS), jnp.bfloat16),
             pltpu.VMEM((M, ROWS), jnp.float32),
             pltpu.VMEM((M, ROWS), jnp.float32),
-            pltpu.VMEM((2 * SLOTS * KL, WAVES), jnp.float32),
+            pltpu.VMEM((2 * SLOTS * KL + KL, WAVES), jnp.float32),
             pltpu.VMEM((KL * WAVES, 128), jnp.float32),
-            pltpu.VMEM((2 * SLOTS * KL, 128), jnp.float32),
+            pltpu.VMEM((2 * SLOTS * KL + KL, 128), jnp.float32),
             pltpu.VMEM((2, GROUP, 4, SH, 128), jnp.bfloat16),
             pltpu.VMEM((2, GROUP, 4, SH, 128), jnp.bfloat16),
             pltpu.VMEM((512, 512), jnp.bfloat16),

time: 42.2 us -> 42.2 us (level)
  no operation moved by 1% of the time
where the time goes in v5:
time: 42.2 us; the launch traced here: 42.1 us
  Pallas kernels  42 us (100%)
    pallas_call x1, Pallas kernels, fields_call(): pl.pallas_call(fields_kernel, out_shape=(jax.ShapeDtypeStruct((M, 2 * SH,...  33 us
    pallas_call x1, Pallas kernels, maps_call(): pl.pallas_call(maps_kernel, out_shape=jax.ShapeDtypeStruct((SH, ROWS, NPH...  9.05 us

profile of v5, /device:TPU:1, one launch (start us, length us, event | category | flops | bytes accessed | tf_op | source)
XLA Modules:
  0.0 42.1 jit_solution(17700838332352867439)
XLA Ops:
  0.0 33.0 %fields.1 = (bf16[256,32,128]{2,1,0:T(8,128)(2,1)S(1)}, bf16[2,256,2048]{2,1,0:T(8,128)(2,1)S(1)}, s32[1,256]{1,0:T(1,128)S(1)}) custom-call(s32[256]{0:T(256)} %mode_hbm.1, s32[1,256]{1,0:T(1,128)} %bitcast.7, s32[16,128]{1,0:T(8,128)} %bitcast.6, f32[256,128]{1,0:T(8,128)} %constant.7.clone.start_hbm, f32[512,128]{1,0:T(8,128)} %constant.8.clone.gain_hbm, ...), custom_call_target="tpu_custom_call" | custom-call | tf_op jit(solution)/shard_map/fields/pallas_call | solution.py:412
  33.0 9.1 %maps.1 = bf16[16,128,4096]{2,1,0:T(8,128)(2,1)} custom-call(s32[1,256]{1,0:T(1,128)S(1)} %get-tuple-element.8.inv_ref, bf16[256,32,128]{2,1,0:T(8,128)(2,1)S(1)} %get-tuple-element.9.f_ref, bf16[2,256,2048]{2,1,0:T(8,128)(2,1)S(1)} %get-tuple-element.10.tab_ref), custom_call_target="tpu_custom_call" | custom-call | tf_op jit(solution)/shard_map/maps/pallas_call | solution.py:386
